TPU v7x, 32 devices: a whole 2x2x4 slice. The times are simulated.
32 devices in a mesh: dp: 8 (over y, x, core), tensor: 4 (over z).
Axes of the slice: x: 2, y: 2, z: 4, core: 2. Of those that a mesh axis runs over, the one named last changes fastest.
Arguments:
- tokens: bfloat16 [128, 256, 768], P(None, 'dp'), may hold values from -6 to 6
- lengths: int32 [256], P('dp'), may hold values from 5 to 128, as said below
- partner: int32 [256], P('dp'), may hold values from 0 to 255, as said below
- w_qkv: bfloat16 [768, 2304], P(None, 'tensor'), may hold values from -0.21875 to 0.21875
- w_out: bfloat16 [768, 768], P('tensor'), may hold values from -0.625 to 0.625
- ln1_gain: float32 [768], replicated, may hold values from 0.25 to 1.75
- ln1_bias: float32 [768], replicated, may hold values from -4 to 4
- up_weight: bfloat16 [768, 3072], P(None, 'tensor'), may hold values from -0.21875 to 0.21875
- up_projection_bias: float32 [3072], P('tensor'), may hold values from -6 to 6
- down_weight: bfloat16 [3072, 768], P('tensor'), may hold values from -0.109375 to 0.109375
- ln2_gain: float32 [768], replicated, may hold values from 0.25 to 1.75
- ln2_bias: float32 [768], replicated, may hold values from -4 to 4
- cot_pooled: bfloat16 [256, 768], P('dp'), may hold values from -6 to 6
- cot_paired: bfloat16 [256, 768], P('dp'), may hold values from -6 to 6
Outputs:
- pooled: bfloat16 [256, 768], P('dp')
- paired: bfloat16 [256, 768], P('dp')
- input_grad: bfloat16 [128, 256, 768], P('tensor', 'dp')
- grad_w_qkv: float32 [768, 2304], P(None, 'tensor')
- grad_w_out: float32 [768, 768], P('tensor')
- grad_ln1_gain: float32 [768], replicated
- grad_ln1_bias: float32 [768], replicated
- grad_w_up: float32 [768, 3072], P(None, 'tensor')
- grad_b_up: float32 [3072], P('tensor')
- grad_w_down: float32 [3072, 768], P('tensor')
- grad_ln2_gain: float32 [768], replicated
- grad_ln2_bias: float32 [768], replicated
Inputs may be any that keep to these rules, and one draw needn't show every extreme that they name: `lengths`: each device's block of 32 sentences holds one of length 128. Sentences come in pairs: partner[partner[s]] = s and partner[s] != s.
All inputs are finite; a program needn't handle non-finite values.
Results may differ from a plain program's by a relative error of at most 0.018.
Values may be sent and summed in bfloat16 or wider, within the bound.
No kernel may reach another device: no remote copies, remote signals or barrier semaphores. Data moves between devices by JAX's collectives and lax.ppermute only.
A program may use at most 256 MiB of HBM per device.

v0:
```python
import functools

import jax
import jax.numpy as jnp
import numpy as np
from jax import lax
from jax.experimental import pallas as pl
from jax.experimental.pallas import tpu as pltpu
from jax.sharding import PartitionSpec as P

HD = 64
EPSILON = 1e-06
LOW = jnp.bfloat16
F32 = jnp.float32
INV_SQRT_2PI = 0.3989422804014327
SQRT_HALF = 0.7071067811865476
TILE = 256
CHUNK = 256
STEP = 16
MASKED = -1000000000.0
LOG2_E = 1.4426950408889634
VMEM_BYTES = 60 * 2**20
NN = (((1,), (0,)), ((), ()))
NT = (((1,), (1,)), ((), ()))
PAIR = 2 * HD
LENS, TILES, LINE, CHOSEN, PLACE, DEST = 16, 32, 33, 40, 48, 80


def mm(a, b, dims=NN):
    return lax.dot_general(a, b, dims, preferred_element_type=F32)


def rows_of(table, s):
    return pl.ds(pl.multiple_of(table[s], 16), 128)


def tile_at(i):
    return pl.ds(pl.multiple_of(i * TILE, TILE), TILE)


def normalize(values):
    center = values - jnp.mean(values, axis=-1, keepdims=True)
    spread = jnp.mean(center * center, axis=-1, keepdims=True)
    root = lax.rsqrt(spread + EPSILON)
    return center * root, root


def normalize_back(z, root, dz):
    return root * (
        dz - jnp.mean(dz, -1, keepdims=True) - z * jnp.mean(dz * z, -1, keepdims=True)
    )


def split_heads(pair):
    first = lax.broadcasted_iota(jnp.int32, pair.shape, 1) < HD
    zero = jnp.zeros_like(pair)
    return jnp.concatenate([jnp.where(first, pair, zero), jnp.where(first, zero, pair)], axis=0)


def join_heads(split):
    n = split.shape[0] // 2
    first = lax.broadcasted_iota(jnp.int32, (n, PAIR), 1) < HD
    return jnp.where(first, split[:n], split[n:])


def place_pieces(table, pieces, slabs, sems):
    copies = []
    for i, piece in enumerate(pieces):
        copies.append(pltpu.make_async_copy(piece, slabs.at[table[PLACE + i]], sems.at[i]))
    return copies


def turn(table, turned, rows, value):
    flat = value.T
    count, slab = turned.shape[0], turned.shape[1]
    for j in range(count):
        turned[table[DEST + j], :, rows] = flat[j * slab : (j + 1) * slab, :]


def pack(table, chosen, tokens, packed, packed_t, x):
    sents, length, width = x.shape
    total = tokens.shape[1]
    depth = total * STEP
    column = lax.broadcasted_iota(jnp.int32, (STEP, depth), 1)
    position = lax.broadcasted_iota(jnp.int32, (STEP, depth), 0)
    here = (column // total) == position
    pick = [here & ((column % total) == chosen[s]) for s in range(sents)]
    pick = jnp.concatenate([jnp.where(item, 1.0, 0.0).astype(LOW) for item in pick], axis=0)
    for block in range(length // STEP):
        rows = slice(block * STEP, (block + 1) * STEP)
        found = mm(pick, tokens[rows].reshape(depth, width)).astype(LOW)
        for s in range(sents):
            x[s, rows, :] = found[s * STEP : (s + 1) * STEP]
    packed[...] = jnp.zeros_like(packed)

    def place(s, _):
        packed[rows_of(table, s), :] = x[s]
        return 0

    lax.fori_loop(0, sents, place, 0)

    def flip(i, _):
        rows = tile_at(i)
        turn(table, packed_t, rows, packed[rows, :])
        return 0

    lax.fori_loop(0, table[TILES], flip, 0)


def send_home(source, *refs):
    blocks, home = refs[:-1], refs[-1]
    share, total, width = home.shape
    depth = total * STEP
    column = lax.broadcasted_iota(jnp.int32, (depth, depth), 1)
    row = lax.broadcasted_iota(jnp.int32, (depth, depth), 0)
    pick = ((column % STEP) == (row // total)) & ((column // STEP) == source[...])
    pick = jnp.where(pick, 1.0, 0.0).astype(LOW)
    for block in range(share // STEP):
        rows = slice(block * STEP, (block + 1) * STEP)
        values = [item[:, rows, :].reshape(-1, width) for item in blocks]
        found = mm(pick, jnp.concatenate(values, axis=0)).astype(LOW)
        home[rows] = found.reshape(STEP, total, width)


def start_all(copies):
    for copy in copies:
        copy.start()


def wait_all(copies):
    for copy in copies:
        copy.wait()


def place_halves(table, orders, arrays, slabs, sems):
    chips, half = slabs.shape[0] // 2, slabs.shape[2] // 2
    copies = []
    for side in range(2):
        for group, order in enumerate(orders):
            columns = slice(0, half) if group < len(orders) // 2 else slice(half, 2 * half)
            source = arrays[side * len(orders) + group]
            for i, m in enumerate(order):
                target = slabs.at[table[PLACE + side * chips + m], :, columns]
                copies.append(
                    pltpu.make_async_copy(source.at[i], target, sems.at[len(copies)])
                )
    return copies


def by_tiles(table, rows, body):
    for n in range(1, rows // TILE + 1):

        @pl.when(table[TILES] == n)
        def _():
            body(n * TILE)


def tile_copies(table, source, target, sems):
    def at(i):
        rows = slice(i * TILE, (i + 1) * TILE)
        return pltpu.make_async_copy(source.at[rows], target.at[rows], sems.at[i])

    def each(act):
        for i in range(sems.shape[0]):

            @pl.when(i < table[TILES])
            def _():
                act(at(i))

    return each


def place_weight(k, steps, weight, own_down, slabs):
    count, slab = slabs.shape[0], slabs.shape[1]
    columns = weight.shape[1]

    @pl.when(k == 0)
    def _():
        weight[:, columns // 2 :] = own_down[...].T

    for t in range(1, steps):

        @pl.when(k == t)
        def _():
            for j in range(count):
                weight[j * slab : (j + 1) * slab, :] = slabs[
                    j, :, (t - 1) * columns : t * columns
                ]


def attention_forward(table, packed, own_qkv, own_out, *refs):
    pieces, refs = refs[:-18], refs[-18:]
    proj_out, ctx_out, probs_out, qkv_out, wo_out, z1_out, root1 = refs[:7]
    proj, ctx, probs, qkv, wo, z1, slabs, sems, out_sems, wide_sems, z1_sems = refs[7:]
    sents, pairs = probs.shape[0], probs.shape[1]
    width = packed.shape[1]
    length = probs.shape[3]
    part = own_out.shape[0]
    block = 4 * part
    heads = part // HD
    arrivals = place_pieces(table, pieces, slabs, sems)
    start_all(arrivals)
    count, slab = slabs.shape[0], slabs.shape[1]
    for h in range(heads):
        for p in range(3):
            source = (h * 3 + p) * HD
            qkv[:, p * width + h * HD : p * width + (h + 1) * HD] = own_qkv[
                source : source + HD, :
            ].T
    wo[:, :part] = own_out[...].T
    ctx[...] = jnp.zeros_like(ctx)
    tiles = table[TILES]
    end = pl.ds(pl.multiple_of(tiles * TILE, TILE), length)
    proj[end, :] = jnp.zeros((length, 3 * width), LOW)
    wait_all(arrivals)
    for j in range(count):
        rows = slice(j * slab, (j + 1) * slab)
        for k in range(1, width // part):
            base = (k - 1) * block
            for p in range(3):
                qkv[rows, p * width + k * part : p * width + (k + 1) * part] = slabs[
                    j, :, base + p * part : base + (p + 1) * part
                ]
            wo[rows, k * part : (k + 1) * part] = slabs[j, :, base + 3 * part : base + block]
    wide_copies = [
        pltpu.make_async_copy(qkv, qkv_out, wide_sems.at[0]),
        pltpu.make_async_copy(wo, wo_out, wide_sems.at[1]),
    ]
    start_all(wide_copies)

    def project(n):
        source = packed[:n, :]
        for c in range(0, 3 * width, CHUNK):
            cols = slice(c, c + CHUNK)
            proj[:n, cols] = mm(source, qkv[:, cols]).astype(LOW)

    by_tiles(table, z1.shape[0], project)
    proj_copy = pltpu.make_async_copy(proj, proj_out, out_sems.at[0])
    proj_copy.start()

    def attend(s, _):
        rows = rows_of(table, s)
        valid = lax.broadcasted_iota(jnp.int32, (length, length), 0) < table[LENS + s]
        for p in range(pairs):
            at = p * PAIR
            queries = proj[rows, at : at + PAIR]
            keys = split_heads(proj[rows, width + at : width + at + PAIR])
            values = split_heads(proj[rows, 2 * width + at : 2 * width + at + PAIR])
            scores = mm(keys, queries, NT)
            for h in range(2):
                half = slice(h * length, (h + 1) * length)
                score = jnp.where(valid, scores[half], MASKED)
                top = jnp.max(score, axis=0, keepdims=True)
                score = jnp.exp2((score - top) * (HD**-0.5 * LOG2_E))
                total = jnp.sum(score, axis=0, keepdims=True)
                probs[s, p, half, :] = (score * (1.0 / total)).astype(LOW)
            ctx[rows, at : at + PAIR] = mm(probs[s, p].T, values).astype(LOW)
        return 0

    lax.fori_loop(0, sents, attend, 0)
    ctx_copies = [
        pltpu.make_async_copy(ctx, ctx_out, out_sems.at[1]),
        pltpu.make_async_copy(probs, probs_out, out_sems.at[2]),
    ]
    start_all(ctx_copies)

    for i in range(z1_sems.shape[0]):
        rows = slice(i * TILE, (i + 1) * TILE)

        @pl.when(i < tiles)
        def _():
            attended = mm(ctx[rows, :], wo[...], NT)
            z, root = normalize(packed[rows, :].astype(F32) + attended)
            z1[rows, :] = z
            root1[rows, :] = jnp.broadcast_to(root, (TILE, 128))
            pltpu.make_async_copy(z1.at[rows], z1_out.at[rows], z1_sems.at[i]).start()

    tile_copies(table, z1, z1_out, z1_sems)(lambda copy: copy.wait())
    wait_all(wide_copies + [proj_copy] + ctx_copies)


def gelu_parts(pre):
    t = pl.reciprocal(1.0 + jnp.abs(pre) * (0.3275911 * SQRT_HALF))
    poly = 0.5 * 1.061405429
    for c in (-1.453152027, 1.421413741, -0.284496736, 0.254829592):
        poly = poly * t + 0.5 * c
    e = jnp.exp2(pre * pre * (-0.5 * LOG2_E))
    tail = poly * t * e
    cdf = jnp.where(pre >= 0.0, 1.0 - tail, tail)
    return pre * cdf, cdf + pre * (e * INV_SQRT_2PI)


def ffn_forward(orders, parts, table, z1_in, gain1, bias1, own_up, own_down_in, bias, gain2, bias2, *refs):
    pieces, refs = refs[:-16], refs[-16:]
    active, slope, z2_out, root2, pooled = refs[:5]
    weight, first, total, z1, z2, own_down, slabs, sems, own_sems, z1_sems, z2_sems = refs[5:]
    k = pl.program_id(0)
    steps = pl.num_programs(0)
    tiles = table[TILES]
    units = active.shape[2]
    arrivals = place_halves(table, orders, pieces, slabs, sems)
    own = [
        pltpu.make_async_copy(own_up, weight.at[:, :units], own_sems.at[0]),
        pltpu.make_async_copy(own_down_in, own_down, own_sems.at[1]),
    ]
    z1_copies = tile_copies(table, z1_in, z1, z1_sems)

    @pl.when(k == 0)
    def _():
        z1_copies(lambda copy: copy.start())
        start_all(own)
        z1_copies(lambda copy: copy.wait())

        def start(i, _):
            rows = tile_at(i)
            value = z1[rows, :] * gain1[...] + bias1[...]
            first[rows, :] = value.astype(LOW)
            total[rows, :] = value
            return 0

        lax.fori_loop(0, tiles, start, 0)
        wait_all(own)
        start_all(arrivals)

    @pl.when(k == 1)
    def _():
        wait_all(arrivals)

    place_weight(k, parts, weight, own_down, slabs)

    def work(n):
        for r in range(0, n, TILE):
            rows = slice(r, r + TILE)
            source = first[rows, :]
            for c in range(0, units, CHUNK):
                cols = slice(c, c + CHUNK)
                act, slp = gelu_parts(mm(source, weight[:, cols]) + bias[0, :, cols])
                active[0, rows, cols] = act.astype(LOW)
                slope[0, rows, cols] = slp.astype(LOW)
            total[rows, :] += mm(active[0, rows, :], weight[:, units:], NT)

    by_tiles(table, first.shape[0], work)

    @pl.when(k == steps - 1)
    def _():
        z2[pl.ds(pl.multiple_of(tiles * TILE, TILE), 128), :] = jnp.zeros((128, z2.shape[1]), F32)

        def finish(i, _):
            rows = tile_at(i)
            z, root = normalize(total[rows, :])
            z2[rows, :] = z
            root2[rows, :] = jnp.broadcast_to(root, (TILE, 128))
            return 0

        lax.fori_loop(0, tiles, finish, 0)
        z2_copies = tile_copies(table, z2, z2_out, z2_sems)
        z2_copies(lambda copy: copy.start())
        means = []
        for s in range(pooled.shape[0]):
            n = table[LENS + s]
            valid = lax.broadcasted_iota(jnp.int32, (128, z2.shape[1]), 0) < n
            rows = jnp.where(valid, z2[rows_of(table, s), :], 0.0)
            means.append(jnp.sum(rows, axis=0, keepdims=True) / n.astype(F32))
        pooled[...] = (jnp.concatenate(means, axis=0) * gain2[...] + bias2[...]).astype(LOW)
        z2_copies(lambda copy: copy.wait())


def weight_grad(table, turned, right, store):
    count, slab, rows = turned.shape

    def body(n):
        if slab % 16 == 0:
            left = turned[:, :, :n].reshape(count * slab, n)
        else:
            left = jnp.concatenate([turned[j, :, :n] for j in range(count)], axis=0)
        store(lambda columns: mm(left, right(n, columns)))

    by_tiles(table, rows, body)


def half_order(chips, bit):
    order = {}
    for m in range(chips):
        order[m] = sum(1 for other in range(m) if (other & bit) == (m & bit))
    return order


def split_send(mine, other, value, k, columns):
    chips, slab = mine.shape[0], mine.shape[2]
    for m in range(chips):
        mine[m, k, :, columns] = value[m * slab : (m + 1) * slab].astype(LOW)
        target, at = other(m)
        target[at, k, :, columns] = value[(chips + m) * slab : (chips + m + 1) * slab].astype(LOW)


def send_chunks(mine, early, late, bit, product):
    order = half_order(mine.shape[0], bit)

    def other(m):
        return (early if m & bit else late), order[m]

    for c in range(0, mine.shape[3], CHUNK):
        cols = slice(c, c + CHUNK)
        split_send(mine, other, product(cols), 0, cols)


def ffn_backward(
    orders, parts, table, pool, z2_in, root2, gain2, z1_in, root1, gain1, bias1, own_up, own_down_in,
    active, slope, *refs
):
    pieces, refs = refs[:-24], refs[-24:]
    down_mine, down_early, down_late, up_mine, up_early, up_late = refs[:6]
    attn_low, attn_t, sums, bias_sum = refs[6:10]
    weight, z1, z2, total, branch, branch_t, first_t, hidden, own_down, slabs = refs[10:20]
    sems, own_sems, z1_sems, z2_sems = refs[20:]
    k = pl.program_id(0)
    tiles = table[TILES]
    width, units = own_up.shape
    arrivals = place_halves(table, orders, pieces, slabs, sems)
    own = [
        pltpu.make_async_copy(own_up, weight.at[:, :units], own_sems.at[0]),
        pltpu.make_async_copy(own_down_in, own_down, own_sems.at[1]),
    ]
    z1_copies = tile_copies(table, z1_in, z1, z1_sems)
    z2_copies = tile_copies(table, z2_in, z2, z2_sems)

    @pl.when(k == 0)
    def _():
        z2_copies(lambda copy: copy.start())
        z1_copies(lambda copy: copy.start())
        start_all(own)
        total[...] = jnp.zeros_like(total)
        for s in range(attn_low.shape[0] // 128):
            n = table[LENS + s]
            valid = lax.broadcasted_iota(jnp.int32, (128, width), 0) < n
            row = pool[pl.ds(table[CHOSEN + s], 1), :] / n.astype(F32)
            total[rows_of(table, s), :] = jnp.where(valid, row, 0.0)
        sums[...] = jnp.zeros_like(sums)
        z2_copies(lambda copy: copy.wait())

        def start(i, _):
            rows = tile_at(i)
            grad = total[rows, :]
            z = z2[rows, :]
            sums[0:1, :] += jnp.sum(grad * z, axis=0, keepdims=True)
            sums[1:2, :] += jnp.sum(grad, axis=0, keepdims=True)
            value = normalize_back(z, root2[rows, 0:1], grad * gain2[...])
            low = value.astype(LOW)
            total[rows, :] = value
            branch[rows, :] = low
            turn(table, branch_t, rows, low)
            return 0

        lax.fori_loop(0, tiles, start, 0)
        z1_copies(lambda copy: copy.wait())

        def flip(i, _):
            rows = tile_at(i)
            turn(table, first_t, rows, (z1[rows, :] * gain1[...] + bias1[...]).astype(LOW))
            return 0

        lax.fori_loop(0, tiles, flip, 0)
        wait_all(own)
        start_all(arrivals)

    @pl.when(k == 1)
    def _():
        wait_all(arrivals)

    place_weight(k, parts, weight, own_down, slabs)
    weight_grad(
        table,
        branch_t,
        lambda n, cols: active[0, :n, cols],
        lambda product: send_chunks(down_mine, down_early, down_late, 1, product),
    )
    bias_sum[...] = jnp.zeros_like(bias_sum)

    def work(n):
        source = branch[:n, :]
        for c in range(0, units, CHUNK):
            cols = slice(c, c + CHUNK)
            grad = mm(source, weight[:, units + c : units + c + CHUNK])
            hid = (slope[0, :n, cols].astype(F32) * grad).astype(LOW)
            hidden[:n, cols] = hid
            bias_sum[0, :, cols] += jnp.sum(hid.astype(F32), axis=0, keepdims=True)
        total[:n, :] += mm(hidden[:n, :], weight[:, :units], NT)

    by_tiles(table, hidden.shape[0], work)
    weight_grad(
        table,
        first_t,
        lambda n, cols: hidden[:n, cols],
        lambda product: send_chunks(
            up_mine, up_early, up_late, up_mine.shape[0] // 2, product
        ),
    )

    @pl.when(k == pl.num_programs(0) - 1)
    def _():
        def finish(i, _):
            rows = tile_at(i)
            grad = total[rows, :]
            z = z1[rows, :]
            sums[2:3, :] += jnp.sum(grad * z, axis=0, keepdims=True)
            sums[3:4, :] += jnp.sum(grad, axis=0, keepdims=True)
            value = normalize_back(z, root1[rows, 0:1], grad * gain1[...])
            low = value.astype(LOW)
            attn_low[rows, :] = low
            turn(table, attn_t, rows, low)
            return 0

        lax.fori_loop(0, tiles, finish, 0)


def attention_backward(table, attn_low, wo, proj_in, probs_in, qkv_in, proj_grad_out, *refs):
    outs, refs = refs[:-7], refs[-7:]
    ctx_grad, proj, probs, qkv, proj_grad, sems, out_sem = refs
    sents, pairs = probs.shape[0], probs.shape[1]
    length = probs.shape[3]
    width = attn_low.shape[1]
    tiles = table[TILES]
    arrivals = [
        pltpu.make_async_copy(proj_in, proj, sems.at[0]),
        pltpu.make_async_copy(probs_in, probs, sems.at[1]),
        pltpu.make_async_copy(qkv_in, qkv, sems.at[2]),
    ]
    start_all(arrivals)
    ctx_grad[...] = jnp.zeros_like(ctx_grad)
    proj_grad[...] = jnp.zeros_like(proj_grad)

    def start(n):
        ctx_grad[:n, :] = mm(attn_low[:n, :], wo[...]).astype(LOW)

    by_tiles(table, attn_low.shape[0], start)
    wait_all(arrivals[:2])
    scale = HD**-0.5

    def attend(s, _):
        rows = rows_of(table, s)
        live = lax.broadcasted_iota(jnp.int32, (length, PAIR), 0) < table[LENS + s]
        for p in range(pairs):
            at = p * PAIR
            queries = proj[rows, at : at + PAIR]
            keys = split_heads(proj[rows, width + at : width + at + PAIR])
            values = split_heads(proj[rows, 2 * width + at : 2 * width + at + PAIR])
            grad = ctx_grad[rows, at : at + PAIR]
            grad = jnp.where(live, grad, jnp.zeros_like(grad))
            prob_grad = mm(values, grad, NT)
            score_grad = []
            for h in range(2):
                half = slice(h * length, (h + 1) * length)
                prob = probs[s, p, half, :].astype(F32)
                part = prob_grad[half]
                inner = jnp.sum(prob * part, axis=0, keepdims=True)
                score_grad.append((prob * (part - inner)).astype(LOW))
            score_grad = jnp.concatenate(score_grad, axis=0)
            proj_grad[rows, at : at + PAIR] = (mm(score_grad.T, keys) * scale).astype(LOW)
            proj_grad[rows, width + at : width + at + PAIR] = (
                join_heads(mm(score_grad, queries)) * scale
            ).astype(LOW)
            proj_grad[rows, 2 * width + at : 2 * width + at + PAIR] = join_heads(
                mm(probs[s, p], grad)
            ).astype(LOW)
        return 0

    lax.fori_loop(0, sents, attend, 0)
    proj_copy = pltpu.make_async_copy(proj_grad, proj_grad_out, out_sem.at[0])
    proj_copy.start()
    arrivals[2].wait()

    def finish(n):
        total = mm(proj_grad[:n, :], qkv[...], NT)
        ctx_grad[:n, :] = (attn_low[:n, :].astype(F32) + total).astype(LOW)

    by_tiles(table, attn_low.shape[0], finish)
    ctx_grad[pl.ds(pl.multiple_of(tiles * TILE, TILE), length), :] = jnp.zeros(
        (length, width), LOW
    )
    share = outs[0].shape[1]
    for k, out in enumerate(outs):
        first = table[LINE + k] * share
        position = lax.broadcasted_iota(jnp.int32, (share, width), 0) + first
        for s in range(sents):
            value = ctx_grad[pl.ds(pl.multiple_of(table[s] + first, 16), share), :]
            out[s] = jnp.where(position < table[LENS + s], value, jnp.zeros_like(value))
    proj_copy.wait()


def attention_weights(table, *refs):
    sources, (mine, other), (packed_t, attn_t, ctx, proj_grad, sems) = refs[:4], refs[4:6], refs[6:]
    width = ctx.shape[1]
    count = mine.shape[1]
    part = width // count
    copies = [
        pltpu.make_async_copy(source, target, sems.at[i])
        for i, (source, target) in enumerate(zip(sources[:3], (packed_t, attn_t, ctx)))
    ]
    for p in range(3):
        cols = slice(p * width, (p + 1) * width)
        copies.append(
            pltpu.make_async_copy(sources[3].at[:, cols], proj_grad.at[:, cols], sems.at[3 + p])
        )
    order = [copies[1], copies[2], copies[0]] + copies[3:]
    start_all(order)

    def store(p, product):
        value = product(slice(p * width, (p + 1) * width) if p < 3 else slice(None))
        for k in range(count):
            split_send(
                mine,
                lambda m: (other, m),
                value[:, k * part : (k + 1) * part],
                k,
                slice(p * part, (p + 1) * part),
            )

    wait_all(order[:2])
    weight_grad(
        table, attn_t, lambda n, cols: ctx[:n, cols], lambda product: store(3, product)
    )
    order[2].wait()
    for p in range(3):
        order[3 + p].wait()
        weight_grad(
            table,
            packed_t,
            lambda n, cols: proj_grad[:n, cols],
            lambda product: store(p, product),
        )


def stacked_pieces(stacks):
    return [stack.at[i] for stack in stacks for i in range(stack.shape[0])]


def place_grads(table, near, far, straight, turned, slabs, flat, sems):
    count, slab = slabs.shape[0], slabs.shape[1]
    arrivals = place_pieces(table, stacked_pieces((near, far)), slabs, sems)
    start_all(arrivals)
    wait_all(arrivals)
    width = straight.shape[1]
    for j in range(count):
        rows = slice(j * slab, (j + 1) * slab)
        straight[rows, :] = slabs[j, :, :width].astype(F32)
        flat[rows, :] = slabs[j, :, width:].astype(F32)
    turned[...] = flat[...].T


def place_attention_grads(table, near, far, qkv, wo, slabs, flat, sems):
    count, slab = slabs.shape[0], slabs.shape[1]
    arrivals = place_pieces(table, stacked_pieces((near, far)), slabs, sems)
    start_all(arrivals)
    wait_all(arrivals)
    for j in range(count):
        flat[j * slab : (j + 1) * slab, :] = slabs[j].astype(F32)
    part = wo.shape[0]
    heads = part // HD
    for p in range(3):
        piece = flat[:, p * part : (p + 1) * part].T
        for h in range(heads):
            target = (h * 3 + p) * HD
            qkv[target : target + HD, :] = piece[h * HD : (h + 1) * HD, :]
    wo[...] = flat[:, 3 * part :].T


COST = 1000000
SMEM = pl.BlockSpec(memory_space=pltpu.SMEM)
VMEM = pl.BlockSpec(memory_space=pltpu.VMEM)
ANY = pl.BlockSpec(memory_space=pl.ANY)


def shape(dims, dtype):
    return jax.ShapeDtypeStruct(dims, dtype)


def params():
    return pltpu.CompilerParams(vmem_limit_bytes=VMEM_BYTES)


def cost(flops, nbytes):
    return pl.CostEstimate(flops=flops // COST, bytes_accessed=nbytes // COST, transcendentals=0)


def add(*terms):
    return sum(term.astype(F32) for term in terms)


def swap(value, mask, axis="dp"):
    return lax.ppermute(value, axis, [(i, i ^ mask) for i in range(lax.axis_size(axis))])


def bits_of(count):
    return [1 << i for i in range(count.bit_length() - 1)]


def take(values, index, axis=0):
    return lax.dynamic_index_in_dim(values, index, axis, False, allow_negative_indices=False)


def cut(values, start, size, axis):
    return lax.dynamic_slice_in_dim(values, start, size, axis, allow_negative_indices=False)


def tie(*values):
    return lax.optimization_barrier(values)


def gather_line(piece):
    n = lax.axis_size("tensor")
    return jnp.concatenate([swap(piece, k, "tensor") for k in range(1, n)], axis=1)


def gather_chips(value):
    return [value] + [swap(value, 2 * m) for m in range(1, lax.axis_size("dp") // 2)]


def gather_cores(near):
    return near + [swap(item, 1) for item in near]


def gather_plane(value):
    return gather_cores(gather_chips(value))


def pick(term, side, bit):
    dims = term.shape
    view = term.reshape((dims[0] // (2 * bit), 2, bit) + dims[1:])[:, side]
    return view.reshape((dims[0] // 2,) + dims[1:])


def sent(terms, bit):
    return add(*[pick(term, 1, bit) for term in terms]).astype(LOW)


def kept(terms, bit, landed):
    return [pick(term, 0, bit) for term in terms] + [landed]


def reduce_line(terms):
    for bit in bits_of(lax.axis_size("tensor")):
        terms = kept(terms, 1, swap(sent(terms, 1), bit, "tensor"))
    return add(*terms)[0].astype(LOW)


def reduce_chips(terms, bits):
    for bit in bits:
        terms = kept(terms, 1, swap(sent(terms, 1), 2 * bit))
    return terms


def shards(
    tokens,
    lengths,
    partner,
    w_qkv,
    w_out,
    ln1_gain,
    ln1_bias,
    up_weight,
    up_projection_bias,
    down_weight,
    ln2_gain,
    ln2_bias,
    cot_pooled,
    cot_paired,
):
    dp_count = lax.axis_size("dp")
    t_count = lax.axis_size("tensor")
    dp_me = lax.axis_index("dp")
    t_me = lax.axis_index("tensor")
    length, sentences, width = tokens.shape
    mine = sentences // t_count
    rows = mine * length
    pad = rows + length
    slab = width // dp_count
    chips = dp_count // 2
    heads = w_qkv.shape[1] // (3 * HD)
    units = up_weight.shape[1]
    ctx_cols = w_out.shape[0]
    block = 4 * ctx_cols

    def by_part(weight):
        return weight.reshape(-1, heads, 3, HD).transpose(0, 2, 1, 3).reshape(weight.shape)

    def rows_piece(weight):
        return cut(weight, dp_me * slab, slab, 0)

    def columns_piece(weight):
        return cut(weight, dp_me * slab, slab, 1).T

    attn_piece = jnp.concatenate([by_part(rows_piece(w_qkv)), columns_piece(w_out)], axis=1)
    attn_piece, up_early, down_early = tie(attn_piece, up_weight, down_weight)
    line_bits = bits_of(t_count)[::-1]

    def widen_line(parts, bit):
        return parts + [swap(jnp.concatenate(parts, axis=1), bit, "tensor")]

    def line_order():
        order = [0]
        for bit in line_bits:
            order += [item ^ bit for item in order]
        return order

    def by_distance(parts, columns):
        wide = jnp.concatenate(parts, axis=1)
        order = line_order()
        return [wide[:, order.index(d) * columns : (order.index(d) + 1) * columns] for d in range(t_count)]

    attn_parts = widen_line([attn_piece], line_bits[0])
    ffn_piece = jnp.concatenate([rows_piece(up_early), columns_piece(down_early)], axis=1)
    attn_parts[1], ffn_piece, up_projection_bias = tie(attn_parts[1], ffn_piece, up_projection_bias)
    for bit in line_bits[1:]:
        attn_parts = widen_line(attn_parts, bit)
    ffn_parts = widen_line([ffn_piece], line_bits[0])
    bias_parts = widen_line([up_projection_bias.reshape(1, units)], line_bits[0])
    attn_line = jnp.concatenate(by_distance(attn_parts, block)[1:], axis=1)

    order = np.arange(sentences)
    ahead = (lengths[None, :] > lengths[:, None]) | (
        (lengths[None, :] == lengths[:, None]) & (order[None, :] < order[:, None])
    )
    rank = jnp.sum(ahead.astype(jnp.int32), axis=1)
    row = rank // t_count
    column = rank % t_count
    column = jnp.where(row % 2 == 0, column, t_count - 1 - column)
    mine_here = (column == t_me)[None, :] & (row[None, :] == order[:mine, None])
    chosen = jnp.sum(jnp.where(mine_here, order[None, :], 0), axis=1)
    counts = jnp.sum(jnp.where(mine_here, lengths[None, :], 0), axis=1)
    source = (column ^ t_me) * mine + row
    taken = (counts + 15) & ~15
    ends = jnp.sum(jnp.where(np.tri(mine, dtype=bool), taken[None, :], 0), axis=1)
    devices = np.arange(dp_count)
    distance = 2 * np.arange(chips)
    near = devices[:, None] ^ distance[None, :]
    spots = np.concatenate([near, near ^ 1], axis=1)
    lines = np.arange(t_count)[:, None] ^ np.arange(t_count)[None, :]
    apart = devices[:, None] ^ devices[None, :]
    fixed = np.zeros((dp_count, DEST - PLACE + dp_count), np.int32)
    fixed[:, :dp_count] = spots
    fixed[:, DEST - PLACE :] = apart % 2 * chips + apart // 2
    line_fixed = np.zeros((t_count, CHOSEN - LINE), np.int32)
    line_fixed[:, :t_count] = lines
    table = jnp.concatenate(
        [
            ends - taken,
            np.zeros(LENS - mine, np.int32),
            counts,
            np.zeros(TILES - LENS - mine, np.int32),
            (ends[-1:] + (TILE - 1)) >> (TILE.bit_length() - 1),
            take(jnp.asarray(line_fixed), t_me),
            chosen,
            np.zeros(PLACE - CHOSEN - mine, np.int32),
            take(jnp.asarray(fixed), dp_me),
        ]
    ).astype(jnp.int32)
    attn_line, chosen = tie(attn_line, chosen)
    turn_shape = shape((dp_count, slab, rows), LOW)
    packed, packed_t = pl.pallas_call(
        pack,
        out_shape=(shape((pad, width), LOW), turn_shape),
        in_specs=[SMEM, SMEM, VMEM],
        out_specs=(VMEM,) * 2,
        scratch_shapes=[pltpu.VMEM((mine, length, width), LOW)],
        compiler_params=params(),
        cost_estimate=cost(0, 8 * rows * width),
        name="pack",
    )(table, chosen, tokens)

    attn_chips = gather_chips(attn_line)
    for bit in line_bits[1:]:
        ffn_parts = widen_line(ffn_parts, bit)
        bias_parts = widen_line(bias_parts, bit)
    bias_all = jnp.stack(by_distance(bias_parts, units))
    *attn_chips, packed = tie(*attn_chips, packed)
    attn_pieces = gather_cores(attn_chips)
    ffn_line = jnp.concatenate(by_distance(ffn_parts, 2 * units)[1:], axis=1)
    middle = ffn_line.shape[1] // 2
    plane_bits = bits_of(chips)
    spread, orders = [], []
    for half, path in ((ffn_line[:, :middle], plane_bits), (ffn_line[:, middle:], plane_bits[::-1])):
        group, order = half[None], [0]
        for bit in path[:-1]:
            group = jnp.concatenate([group, swap(group, 2 * bit)])
            order = order + [item ^ bit for item in order]
        spread.append(group)
        orders += [order, [item ^ path[-1] for item in order]]
    attn_pieces[0], bias_all, *spread = tie(attn_pieces[0], bias_all, *spread)
    later = [swap(spread[0], 2 * plane_bits[-1]), swap(spread[1], 2 * plane_bits[0])]
    pairs = width // PAIR
    probs_shape = (mine, pairs, 2 * length, length)
    proj, ctx, probs, qkv, wo, z1, root1 = pl.pallas_call(
        attention_forward,
        out_shape=(
            shape((pad, 3 * width), LOW),
            shape((pad, width), LOW),
            shape(probs_shape, LOW),
            shape((width, 3 * width), LOW),
            shape((width, width), LOW),
            shape((rows, width), F32),
            shape((rows, 128), F32),
        ),
        in_specs=[SMEM, VMEM, VMEM, VMEM] + [ANY] * dp_count,
        out_specs=(ANY,) * 6 + (VMEM,),
        scratch_shapes=[
            pltpu.VMEM((pad, 3 * width), LOW),
            pltpu.VMEM((pad, width), LOW),
            pltpu.VMEM(probs_shape, LOW),
            pltpu.VMEM((width, 3 * width), LOW),
            pltpu.VMEM((width, width), LOW),
            pltpu.VMEM((rows, width), F32),
            pltpu.VMEM((dp_count, slab, (t_count - 1) * block), LOW),
            pltpu.SemaphoreType.DMA((dp_count,)),
            pltpu.SemaphoreType.DMA((3,)),
            pltpu.SemaphoreType.DMA((2,)),
            pltpu.SemaphoreType.DMA((rows // TILE,)),
        ],
        compiler_params=params(),
        cost_estimate=cost(8 * rows * width * width, 30 * rows * width),
        name="attention_forward",
    )(table, packed, w_qkv.T, w_out, *attn_pieces)
    *later, z1 = tie(*later, z1)
    ffn_pieces = [spread[0], later[0], spread[1], later[1]]
    ffn_pieces += [swap(item, 1) for item in ffn_pieces]

    gain1, bias1 = ln1_gain.reshape(1, width), ln1_bias.reshape(1, width)
    gain2, bias2 = ln2_gain.reshape(1, width), ln2_bias.reshape(1, width)

    def whole(*dims):
        return pl.BlockSpec(dims, lambda k, table: (0,) * len(dims))

    def call(kernel, outs, ins, out_specs, scratch, flops, nbytes):
        return pl.pallas_call(
            functools.partial(kernel, orders, t_count),
            out_shape=outs,
            grid_spec=pltpu.PrefetchScalarGridSpec(
                num_scalar_prefetch=1,
                grid=(t_count,),
                in_specs=ins,
                out_specs=out_specs,
                scratch_shapes=scratch,
            ),
            compiler_params=params(),
            cost_estimate=cost(flops, nbytes),
            name=kernel.__name__,
        )

    act_spec = pl.BlockSpec((1, rows, units), lambda k, table: (k, 0, 0))
    bias_spec = pl.BlockSpec((1, 1, units), lambda k, table: (k, 0, 0))
    line = whole(1, width)
    full = whole(rows, width)
    root_spec = whole(rows, 128)
    act_shape = shape((t_count, rows, units), LOW)
    weight_scratch = [
        pltpu.VMEM((units, width), LOW),
        pltpu.VMEM((dp_count, slab, (t_count - 1) * 2 * units), LOW),
        pltpu.SemaphoreType.DMA((2 * dp_count,)),
        pltpu.SemaphoreType.DMA((2,)),
        pltpu.SemaphoreType.DMA((rows // TILE,)),
        pltpu.SemaphoreType.DMA((rows // TILE,)),
    ]
    active, slope, z2, root2, pooled = call(
        ffn_forward,
        (
            act_shape,
            act_shape,
            shape((rows, width), F32),
            shape((rows, 128), F32),
            shape((mine, width), LOW),
        ),
        [ANY, line, line, ANY, ANY, bias_spec, line, line] + [ANY] * len(ffn_pieces),
        (act_spec, act_spec, ANY, root_spec, whole(mine, width)),
        [
            pltpu.VMEM((width, 2 * units), LOW),
            pltpu.VMEM((rows, width), LOW),
            pltpu.VMEM((rows, width), F32),
            pltpu.VMEM((rows, width), F32),
            pltpu.VMEM((pad, width), F32),
        ]
        + weight_scratch,
        4 * rows * width * units * t_count,
        40 * rows * width,
    )(table, z1, gain1, bias1, up_weight, down_weight, bias_all, gain2, bias2, *ffn_pieces)

    line_pooled = jnp.stack([pooled] + [swap(pooled, k, "tensor") for k in range(1, t_count)])
    returned = line_pooled.reshape(sentences, width)[source]
    both = jnp.concatenate([returned, cot_paired])
    everyone = jnp.stack(gather_plane(both)).reshape(-1, width)
    apart = (partner // sentences) ^ dp_me
    base = ((apart & 1) * chips + (apart >> 1)) * (2 * sentences) + partner % sentences
    partner_pooled = everyone[base].astype(F32)
    partner_cot = everyone[base + sentences].astype(F32)
    paired = (returned.astype(F32) * partner_pooled).astype(LOW)
    pool_grad = cot_pooled.astype(F32) + partner_pooled * (cot_paired.astype(F32) + partner_cot)
    pool_grad = pool_grad.astype(LOW).astype(F32)

    send_spec = pl.BlockSpec((chips, 1, slab, units), lambda k, table: (0, k, 0, 0))
    send_shape = shape((chips, t_count, slab, units), LOW)
    half_spec = pl.BlockSpec((chips // 2, 1, slab, units), lambda k, table: (0, k, 0, 0))
    half_shape = shape((chips // 2, t_count, slab, units), LOW)
    down_mine, down_early, down_late, up_mine, up_early, up_late, *small_parts = call(
        ffn_backward,
        (send_shape, half_shape, half_shape) * 2
        + (
            shape((rows, width), LOW),
            turn_shape,
            shape((4, width), F32),
            shape((t_count, 1, units), F32),
        ),
        [whole(sentences, width), ANY, root_spec, line, ANY, root_spec, line, line, ANY, ANY]
        + [act_spec, act_spec]
        + [ANY] * len(ffn_pieces),
        (send_spec, half_spec, half_spec) * 2
        + (full, whole(dp_count, slab, rows), whole(4, width), bias_spec),
        [
            pltpu.VMEM((width, 2 * units), LOW),
            pltpu.VMEM((rows, width), F32),
            pltpu.VMEM((rows, width), F32),
            pltpu.VMEM((pad, width), F32),
            pltpu.VMEM((rows, width), LOW),
            pltpu.VMEM((dp_count, slab, rows), LOW),
            pltpu.VMEM((dp_count, slab, rows), LOW),
            pltpu.VMEM((rows, units), LOW),
        ]
        + weight_scratch,
        8 * rows * width * units * t_count,
        60 * rows * width,
    )(
        table, pool_grad, z2, root2, gain2, z1, root1, gain1, bias1, up_weight, down_weight,
        active, slope, *ffn_pieces
    )

    attn_low, attn_t, sums, bias_sum = small_parts

    def small_step(norms, bias_part, mask):
        half = bias_part.shape[0] // 2
        split = bias_part.reshape(half, 2, units)
        got = swap(jnp.concatenate([split[:, 1], norms]), mask, "tensor")
        return norms, got, split[:, 0]

    def small_sum(norms, got, bias_part):
        half = bias_part.shape[0]
        return norms + got[half:], bias_part + got[:half]

    chip_bits = bits_of(chips)
    high = chip_bits[-1]
    down_early, up_early = swap(down_early, 1), swap(up_early, 1)
    small = jnp.concatenate([bias_sum.reshape(t_count, units), sums])
    small = small + swap(small, 1)
    down_sent, up_sent, small, attn_low = tie(
        add(pick(down_mine, 1, 1), down_early).astype(LOW),
        add(pick(up_mine, 1, high), up_early).astype(LOW),
        small,
        attn_low,
    )
    down_got, up_got = swap(down_sent, 2), swap(up_sent, 2 * high)
    down_late, up_late, small, attn_t = tie(down_late, up_late, small, attn_t)
    norms, small_got, bias_part = small_step(small[t_count:], small[:t_count], 1)
    down_late, up_late = swap(down_late, 1), swap(up_late, 1)

    share = length // t_count
    proj_grad, *input_blocks = pl.pallas_call(
        attention_backward,
        out_shape=(shape((pad, 3 * width), LOW),)
        + (shape((mine, share, width), LOW),) * t_count,
        in_specs=[SMEM, VMEM, VMEM, ANY, ANY, ANY],
        out_specs=(ANY,) + (VMEM,) * t_count,
        scratch_shapes=[
            pltpu.VMEM((pad, width), LOW),
            pltpu.VMEM((pad, 3 * width), LOW),
            pltpu.VMEM(probs_shape, LOW),
            pltpu.VMEM((width, 3 * width), LOW),
            pltpu.VMEM((pad, 3 * width), LOW),
            pltpu.SemaphoreType.DMA((3,)),
            pltpu.SemaphoreType.DMA((1,)),
        ],
        compiler_params=params(),
        cost_estimate=cost(12 * rows * width * width, 30 * rows * width),
        name="attention_backward",
    )(table, attn_low, wo, proj, probs, qkv)

    down_got, up_got, down_late, up_late, small_got, proj_grad, *input_blocks = tie(
        down_got, up_got, down_late, up_late, small_got, proj_grad, *input_blocks
    )
    norms, bias_part = small_sum(norms, small_got, bias_part)
    down_terms = [pick(down_mine, 0, 1), down_late, down_got]
    up_terms = [pick(up_mine, 0, high), up_late, up_got]
    for low, top in zip(chip_bits[1:-1], chip_bits[1:-1][::-1]):
        down_terms = kept(down_terms, 1, swap(sent(down_terms, 1), 2 * low))
        up_terms = kept(up_terms, top, swap(sent(up_terms, top), 2 * top))
    down_sent, up_sent, norms, proj_grad, *input_blocks = tie(
        sent(down_terms, 1), sent(up_terms, 1), norms, proj_grad, *input_blocks
    )
    norms, small_got, bias_part = small_step(norms, bias_part, 2)
    down_got, up_got = swap(down_sent, 2 * high), swap(up_sent, 2)
    input_landed = [input_blocks[0]] + [None] * (t_count - 1)
    input_landed[2] = swap(input_blocks[2], 2, "tensor")
    input_landed[1] = swap(input_blocks[1], 1, "tensor")

    attn_mine, attn_other = pl.pallas_call(
        attention_weights,
        out_shape=(shape((chips, t_count, slab, block), LOW),) * 2,
        in_specs=[SMEM] + [ANY] * 4,
        out_specs=(VMEM,) * 2,
        scratch_shapes=[
            pltpu.VMEM((dp_count, slab, rows), LOW),
            pltpu.VMEM((dp_count, slab, rows), LOW),
            pltpu.VMEM((pad, width), LOW),
            pltpu.VMEM((pad, 3 * width), LOW),
            pltpu.SemaphoreType.DMA((6,)),
        ],
        compiler_params=params(),
        cost_estimate=cost(8 * rows * width * width, 30 * rows * width),
        name="attention_weights",
    )(table, packed_t, attn_t, ctx, proj_grad)

    def finish(kernel, near, outs, flat):
        near = jnp.stack(near)
        far = swap(near, 1)
        return pl.pallas_call(
            kernel,
            out_shape=tuple(shape(dims, F32) for dims in outs),
            in_specs=[SMEM, ANY, ANY],
            out_specs=(VMEM,) * 2,
            scratch_shapes=[
                pltpu.VMEM((dp_count,) + near.shape[1:], LOW),
                pltpu.VMEM((width, flat), F32),
                pltpu.SemaphoreType.DMA((dp_count,)),
            ],
            compiler_params=params(),
            cost_estimate=cost(0, 8 * width * near.shape[2]),
            name=kernel.__name__,
        )(table, near, far)

    attn_other, small_got, down_got, up_got, input_landed[1], input_landed[2] = tie(
        attn_other, small_got, down_got, up_got, input_landed[1], input_landed[2]
    )
    norms, bias_part = small_sum(norms, small_got, bias_part)
    small = jnp.concatenate([bias_part, norms])
    attn_got = swap(attn_other, 1)
    attn_sent = [add(attn_mine[m], attn_got[m]).astype(LOW) for m in range(1, chips)]
    ffn_line = jnp.concatenate(
        [add(*kept(up_terms, 1, up_got))[0], add(*kept(down_terms, 1, down_got))[0]], axis=2
    )
    ffn_line = [ffn_line.astype(LOW)]
    ffn_sent, small, *attn_sent = tie(sent(ffn_line, 1), small, *attn_sent)
    attn_got = [attn_got[0]] + [swap(item, 2 * m) for m, item in zip(range(1, chips), attn_sent)]
    ffn_got = swap(ffn_sent, 1, "tensor")
    small_got = swap(small, 2)

    ffn_line = kept(ffn_line, 1, ffn_got)
    ffn_got = swap(sent(ffn_line, 1), 2, "tensor")
    *attn_got, ffn_got, small_got = tie(*attn_got, ffn_got, small_got)
    small = small + small_got
    attn_line = [add(attn_mine[0], *attn_got).astype(LOW)]
    ffn_sum = add(*kept(ffn_line, 1, ffn_got))[0].astype(LOW)
    attn_sent, ffn_sum, small = tie(sent(attn_line, 1), ffn_sum, small)
    small_got = swap(small, 4)
    attn_got = swap(attn_sent, 1, "tensor")
    ffn_chips = gather_chips(ffn_sum)
    attn_line = kept(attn_line, 1, attn_got)
    attn_got = swap(sent(attn_line, 1), 2, "tensor")
    attn_got, small_got, input_blocks[3], *ffn_chips = tie(
        attn_got, small_got, input_blocks[3], *ffn_chips
    )
    small = small + small_got
    for mask in bits_of(dp_count)[3:]:
        small = small + swap(small, mask)
    attn_sum = add(*kept(attn_line, 1, attn_got))[0].astype(LOW)
    attn_sum, input_blocks[3], ffn_chips[0] = tie(attn_sum, input_blocks[3], ffn_chips[0])
    attn_chips = gather_chips(attn_sum)
    input_landed[3] = swap(input_blocks[3], 3, "tensor")
    up_grad, down_grad = finish(place_grads, ffn_chips, ((width, units), (units, width)), units)
    attn_chips[0], up_grad, input_landed[3] = tie(attn_chips[0], up_grad, input_landed[3])
    qkv_grad, out_grad = finish(
        place_attention_grads, attn_chips, ((3 * ctx_cols, width), (ctx_cols, width)), block
    )
    home = pl.pallas_call(
        send_home,
        out_shape=shape((share, sentences, width), LOW),
        in_specs=[VMEM] * (1 + t_count),
        out_specs=VMEM,
        compiler_params=params(),
        cost_estimate=cost(0, 4 * share * sentences * width),
        name="send_home",
    )(jnp.tile(source, STEP).reshape(-1, 1), *input_landed)
    bias_sum, norms = small[0], small[1:]
    return (
        returned,
        paired,
        home,
        qkv_grad.T,
        out_grad,
        norms[2],
        norms[3],
        up_grad,
        bias_sum,
        down_grad,
        norms[0],
        norms[1],
    )


def solution(mesh):
    placed = (
        P(None, "dp", None),
        P("dp"),
        P("dp"),
        P(None, "tensor"),
        P("tensor", None),
        P(),
        P(),
        P(None, "tensor"),
        P("tensor"),
        P("tensor", None),
        P(),
        P(),
        P("dp", None),
        P("dp", None),
    )
    return jax.shard_map(
        shards,
        mesh=mesh,
        in_specs=placed,
        out_specs=(
            P("dp", None),
            P("dp", None),
            P("tensor", "dp", None),
            P(None, "tensor"),
            P("tensor", None),
            P(),
            P(),
            P(None, "tensor"),
            P("tensor"),
            P("tensor", None),
            P(),
            P(),
        ),
        check_vma=False,
    )
```

profile of v0, /device:TPU:9, one launch (start us, length us, event | category | flops | bytes accessed | tf_op | source)
XLA Modules:
  0.0 327.7 jit_solution(9646585481634586240)
XLA Ops:
  0.7 1.2 constant_dynamic-slice_fusion.2
  2.0 1.0 constant_dynamic-slice_fusion.1
  3.2 2.4 collective-permute-start
  6.3 0.9 constant_dynamic-slice_fusion
  7.8 4.4 %collective-permute-done = bf16[96,768]{1,0:T(8,128)(2,1)S(1)} collective-permute-done((bf16[96,768]{1,0:T(8,128)(2,1)S(1)}, bf16[96,768]{1,0:T(8,128)(2,1)S(1)}, u32[]{:S(2)}, u32[]{:S(2)}) %collective-permute-start) | collective-permute-done | bytes 147488 | tf_op jit(solution)/shard_map/ppermute | solution.py:690
  12.2 3.1 collective-permute-start.7
  16.2 9.2 %collective-permute-done.7 = bf16[96,1536]{1,0:T(8,128)(2,1)S(1)} collective-permute-done((bf16[96,1536]{1,0:T(8,128)(2,1)S(1)}, bf16[96,1536]{1,0:T(8,128)(2,1)S(1)}, u32[]{:S(2)}, u32[]{:S(2)}) %collective-permute-start.7) | collective-permute-done | bytes 294944 | tf_op jit(solution)/shard_map/ppermute | solution.py:690
  25.4 1.8 collective-permute-start.8
  27.2 1.2 collective-permute-done.5
  28.6 1.3 collective-permute-start.2
  29.8 1.1 collective-permute-start.3
  31.3 7.4 %collective-permute-done.8 = bf16[96,3072]{1,0:T(8,128)(2,1)S(1)} collective-permute-done((bf16[96,3072]{1,0:T(8,128)(2,1)S(1)}, bf16[96,3072]{1,0:T(8,128)(2,1)S(1)}, u32[]{:S(2)}, u32[]{:S(2)}) %collective-permute-start.8) | collective-permute-done | bytes 589856 | tf_op jit(solution)/shard_map/ppermute | solution.py:690
  42.0 1.1 collective-permute-start.9
  43.7 6.2 %pack.1 = (bf16[1152,768]{1,0:T(8,128)(2,1)}, bf16[8,96,1024]{2,1,0:T(8,128)(2,1)}) custom-call(s32[88]{0:T(128)} %concatenate.64.table, s32[8]{0:T(128)} %copy-done.27, bf16[128,32,768]{2,1,0:T(8,128)(2,1)} %tokens.1), custom_call_target="tpu_custom_call" | custom-call | bytes 6 | tf_op jit(solution)/shard_map/pack/pallas_call | solution.py:859
  50.0 3.7 %collective-permute-start.13 = (bf16[96,2304]{1,0:T(8,128)(2,1)S(1)}, bf16[96,2304]{1,0:T(8,128)(2,1)S(1)}, u32[]{:S(2)}, u32[]{:S(2)}) collective-permute-start(bf16[96,2304]{1,0:T(8,128)(2,1)S(1)} %pad_maximum_fusion.8.refs_0_), channel_id=1, source_target_pairs={{0,4},{4,0},{8,12},{12,8},{16,20},{20,16},{24,28},{28,24},{1,5},{5... | collective-permute-start | bytes 1327112 | tf_op jit(solution)/shard_map/ppermute | solution.py:690
  53.7 6.1 %collective-permute-done.10 = bf16[1,96,2304]{2,1,0:T(8,128)(2,1)S(1)} collective-permute-done((bf16[1,96,2304]{2,1,0:T(8,128)(2,1)S(1)}, bf16[1,96,2304]{2,1,0:T(8,128)(2,1)S(1)}, u32[]{:S(2)}, u32[]{:S(2)}) %collective-permute-start.10) | collective-permute-done | bytes 442400 | tf_op jit(solution)/shard_map/ppermute | solution.py:690
  60.4 1.1 collective-permute-start.12
  61.6 2.2 collective-permute-start.14
  64.2 1.1 collective-permute-done.14.refs_5_
  67.7 19.1 %attention_forward.1 = (bf16[1152,2304]{1,0:T(8,128)(2,1)}, bf16[1152,768]{1,0:T(8,128)(2,1)}, bf16[8,6,256,128]{3,2,1,0:T(8,128)(2,1)}, bf16[768,2304]{1,0:T(8,...) custom-call(s32[88]{0:T(128)} %concatenate.64.table, ...), custom_call_target="tpu_custom_call" | custom-call | flops 4831 | bytes 23 | tf_op jit(solution)/shard_map/attention_forward/pallas_call | solution.py:892
  89.9 1.0 copy-done.6
  90.9 22.9 %ffn_forward.1 = (bf16[4,1024,768]{2,1,0:T(8,128)(2,1)}, bf16[4,1024,768]{2,1,0:T(8,128)(2,1)}, f32[1024,768]{1,0:T(8,128)}, f32[1024,128]{1,0:T(8,128)}, bf16[8,768]{1,0:T(8,128)(2,1)}) custom-call(s32[88]{0:T(128)} %concatenate.64.table, f32[1024,768]{1,0:T(8,128)} %get-tuple-element.144.z1_in, f32[1,768]{1,0:T(1,128)} %reshape.678.gain1, ...), custom_call_target="tpu_custom_call" | custom-call | flops 9663 | bytes 31 | tf_op jit(solution)/shard_map/ffn_forward/pallas_call | solution.py:962
  113.8 1.5 collective-permute-start.21
  116.6 2.4 collective-permute-done.22
  120.5 1.1 collective-permute-start.24
  122.1 1.2 collective-permute-start.26
  123.3 2.6 collective-permute-start.27
  125.8 1.9 collective-permute-start.28
  128.7 1.0 collective-permute-start.30
  132.7 41.1 %ffn_backward.1 = (bf16[4,4,96,768]{3,2,1,0:T(8,128)(2,1)}, bf16[2,4,96,768]{3,2,1,0:T(8,128)(2,1)}, bf16[2,4,96,768]{3,2,1,0:T(8,128)(2,1)}, bf16[4,4,96,768]{3...) custom-call(s32[88]{0:T(128)} %concatenate.64.table, ...), custom_call_target="tpu_custom_call" | custom-call | flops 19327 | bytes 47 | tf_op jit(solution)/shard_map/ffn_backward/pallas_call | solution.py:1001
  176.2 2.2 collective-permute-done.33
  179.2 1.7 fusion
  181.2 1.3 fusion.1
  184.8 3.4 %collective-permute-start.38 = (f32[6,768]{1,0:T(8,128)S(1)}, f32[6,768]{1,0:T(8,128)S(1)}, u32[]{:S(2)}, u32[]{:S(2)}) collective-permute-start(f32[6,768]{1,0:T(8,128)S(1)} %pad_maximum_fusion.13), channel_id=1, source_target_pairs={{0,1},{1,0},{2,3},{3,2},{4,5},{5,4},{6,7},{7,6},{8,9},{9,8},{10,11... | collective-permute-start | bytes 55304 | tf_op jit(solution)/shard_map/ppermute | solution.py:690
  188.2 1.3 slice_bitcast_fusion.3
  189.6 21.4 %attention_backward.1 = (bf16[1152,2304]{1,0:T(8,128)(2,1)}, bf16[8,32,768]{2,1,0:T(8,128)(2,1)}, bf16[8,32,768]{2,1,0:T(8,128)(2,1)}, bf16[8,32,768]{2,1,0:T(8,128)(2,1)}, bf16[8,32,768]{2,1,0:T(8,128)(2,1)}) custom-call(s32[88]{0:T(128)} %concatenate.64.table, bf16[1024,768]{1,0:T(8,128)(2,1)} %get-tuple-element.170.attn_low, ...), custom_call_target="tpu_custom_call" | custom-call | flops 7247 | bytes 23 | tf_op jit(solution)/shard_map/attention_backward/pallas_call | solution.py:1062
  211.0 2.3 fusion.17
  213.3 2.3 fusion.13
  217.2 3.3 %collective-permute-start.42 = (bf16[8,32,768]{2,1,0:T(8,128)(2,1)}, bf16[8,32,768]{2,1,0:T(8,128)(2,1)S(1)}, u32[]{:S(2)}, u32[]{:S(2)}) collective-permute-start(bf16[8,32,768]{2,1,0:T(8,128)(2,1)} %get-tuple-element.199), channel_id=1, source_target_pairs={{0,1},{1,0},{2,3},{3,2},{4,5},{5,4},{6,7},{7,6},{8,9},{9,8},{10,11... | collective-permute-start | bytes 1179656 | tf_op jit(solution)/shard_map/ppermute | solution.py:690
  220.8 2.3 collective-permute-start.39
  223.0 9.8 %attention_weights.1 = (bf16[4,4,96,768]{3,2,1,0:T(8,128)(2,1)}, bf16[4,4,96,768]{3,2,1,0:T(8,128)(2,1)}) custom-call(s32[88]{0:T(128)} %concatenate.64.table, bf16[8,96,1024]{2,1,0:T(8,128)(2,1)} %get-tuple-element.191.refs_0_, bf16[8,96,1024]{2,1,0:T(8,128)(2,1)} %get-tuple-element.192.refs_1_, bf16[1152,768]{1,0:T(8,128)(2,1)} %get-tuple-element.193.refs_2_, ...), custom_call_target="tpu_custom_call" | custom-call | flops 4831 | bytes 23 | tf_op jit(solution)/shard_map/attention_weights/pallas_call | solution.py:1100
  232.8 4.6 %collective-permute-done.39 = f32[5,768]{1,0:T(8,128)S(1)} collective-permute-done((f32[5,768]{1,0:T(8,128)S(1)}, f32[5,768]{1,0:T(8,128)S(1)}, u32[]{:S(2)}, u32[]{:S(2)}) %collective-permute-start.39) | collective-permute-done | bytes 15392 | tf_op jit(solution)/shard_map/ppermute | solution.py:690
  237.4 2.7 collective-permute-start.44
  240.2 1.5 fusion.7
  241.7 1.5 fusion.4
  243.4 1.1 collective-permute-done.44
  245.5 2.7 collective-permute-start.48
  249.4 1.5 collective-permute-start.47
  250.9 11.0 %collective-permute-done.48 = bf16[2,96,1536]{2,1,0:T(8,128)(2,1)S(1)} collective-permute-done((bf16[2,96,1536]{2,1,0:T(8,128)(2,1)S(1)}, bf16[2,96,1536]{2,1,0:T(8,128)(2,1)S(1)}, u32[]{:S(2)}, u32[]{:S(2)}) %collective-permute-start.48) | collective-permute-done | bytes 589856 | tf_op jit(solution)/shard_map/ppermute | solution.py:690
  262.0 1.5 collective-permute-start.49
  264.0 12.0 %collective-permute-done.50 = f32[5,768]{1,0:T(8,128)S(1)} collective-permute-done((f32[5,768]{1,0:T(8,128)S(1)}, f32[5,768]{1,0:T(8,128)S(1)}, u32[]{:S(2)}, u32[]{:S(2)}) %collective-permute-start.50) | collective-permute-done | bytes 15392 | tf_op jit(solution)/shard_map/ppermute | solution.py:690
  277.0 3.0 collective-permute-start.51
  281.2 1.5 collective-permute-start.56
  282.6 4.3 %collective-permute-done.51 = bf16[2,96,768]{2,1,0:T(8,128)(2,1)S(1)} collective-permute-done((bf16[2,96,768]{2,1,0:T(8,128)(2,1)S(1)}, bf16[2,96,768]{2,1,0:T(8,128)(2,1)S(1)}, u32[]{:S(2)}, u32[]{:S(2)}) %collective-permute-start.51) | collective-permute-done | bytes 294944 | tf_op jit(solution)/shard_map/ppermute | solution.py:690
  287.0 1.4 collective-permute-start.52
  289.3 6.8 %collective-permute-done.53 = f32[5,768]{1,0:T(8,128)S(1)} collective-permute-done((f32[5,768]{1,0:T(8,128)S(1)}, f32[5,768]{1,0:T(8,128)S(1)}, u32[]{:S(2)}, u32[]{:S(2)}) %collective-permute-start.53) | collective-permute-done | bytes 15392 | tf_op jit(solution)/shard_map/ppermute | solution.py:690
  299.4 1.2 collective-permute-start.61
  300.6 1.0 copy-done.12
  301.6 4.9 %place_grads.1 = (f32[768,768]{1,0:T(8,128)}, f32[768,768]{1,0:T(8,128)}) custom-call(s32[88]{0:T(128)} %concatenate.64.table, bf16[4,96,1536]{2,1,0:T(8,128)(2,1)} %copy-done.3, bf16[4,96,1536]{2,1,0:T(8,128)(2,1)} %copy-done.12), custom_call_target="tpu_custom_call" | custom-call | bytes 9 | tf_op jit(solution)/shard_map/place_grads/pallas_call | solution.py:1120
  306.5 9.0 %collective-permute-done.58.refs_3_ = bf16[8,32,768]{2,1,0:T(8,128)(2,1)S(1)} collective-permute-done((bf16[8,32,768]{2,1,0:T(8,128)(2,1)S(1)}, bf16[8,32,768]{2,1,0:T(8,128)(2,1)S(1)}, u32[]{:S(2)}, u32[]{:S(2)}) %collective-permute-start.58) | collective-permute-done | bytes 393248 | tf_op jit(solution)/shard_map/ppermute | solution.py:690
  315.7 1.7 collective-permute-start.62
  317.4 1.0 reshape_tile.4.source
  319.0 3.6 %send_home.1 = bf16[32,32,768]{2,1,0:T(8,128)(2,1)} custom-call(s32[512,1]{1,0:T(8,128)} %reshape_tile.4.source, bf16[8,32,768]{2,1,0:T(8,128)(2,1)} %get-tuple-element.190.refs_0_, bf16[8,32,768]{2,1,0:T(8,128)(2,1)} %copy-done.19, bf16[8,32,768]{2,1,0:T(8,128)(2,1)} %collective-permute-done.43.refs_2_, bf16[8,32,768]{2,1,0:T(8,128)(2,1)} %copy-done.20), custom_call_target="tpu_custom_call" | custom-call | bytes 3 | tf_op jit(solution)/shard_map/send_home/pallas_call | solution.py:1178
  323.4 4.1 %place_attention_grads.1 = (f32[576,768]{1,0:T(8,128)}, f32[192,768]{1,0:T(8,128)}) custom-call(s32[88]{0:T(128)} %concatenate.64.table, bf16[4,96,768]{2,1,0:T(8,128)(2,1)} %copy-done.9, bf16[4,96,768]{2,1,0:T(8,128)(2,1)} %copy-done.13), custom_call_target="tpu_custom_call" | custom-call | bytes 4 | tf_op jit(solution)/shard_map/place_attention_grads/pallas_call | solution.py:1120
  (241 shorter events, 38.0 us)
Async XLA Ops:
  3.2 9.0 %collective-permute-start = (bf16[96,768]{1,0:T(8,128)(2,1)S(1)}, bf16[96,768]{1,0:T(8,128)(2,1)S(1)}, u32[]{:S(2)}, u32[]{:S(2)}) collective-permute-start(bf16[96,768]{1,0:T(8,128)(2,1)S(1)} %pad_maximum_fusion.11), channel_id=1, source_target_pairs={{0,2},{1,3},{2,0},{3,1},{4,6},{5,7},{6,4},{7,5},{8,10},{9,11},{10,... | collective-permute-start | bytes 442376 | tf_op jit(solution)/shard_map/ppermute | solution.py:690
  7.6 33.7 %copy-start.27 = (s32[8]{0:T(128)}, s32[8]{0:T(128)S(1)}, u32[]{:S(2)}) copy-start(s32[8]{0:T(128)S(1)} %get-tuple-element.131.chosen) | copy-start | bytes 100
  12.2 13.1 %collective-permute-start.7 = (bf16[96,1536]{1,0:T(8,128)(2,1)S(1)}, bf16[96,1536]{1,0:T(8,128)(2,1)S(1)}, u32[]{:S(2)}, u32[]{:S(2)}) collective-permute-start(bf16[96,1536]{1,0:T(8,128)(2,1)S(1)} %pad_maximum_fusion.9), channel_id=1, source_target_pairs={{0,2},{1,3},{2,0},{3,1},{4,6},{5,7},{6,4},{7,5},{8,10},{9,11},{10,... | collective-permute-start | bytes 884744 | tf_op jit(solution)/shard_map/ppermute | solution.py:690
  16.0 12.5 %collective-permute-start.1 = (bf16[96,1536]{1,0:T(8,128)(2,1)S(1)}, bf16[96,1536]{1,0:T(8,128)(2,1)S(1)}, u32[]{:S(2)}, u32[]{:S(2)}) collective-permute-start(bf16[96,1536]{1,0:T(8,128)(2,1)S(1)} %pad_maximum_fusion.10), channel_id=1, source_target_pairs={{0,1},{1,0},{2,3},{3,2},{4,5},{5,4},{6,7},{7,6},{8,9},{9,8},{10,11... | collective-permute-start | bytes 884744 | tf_op jit(solution)/shard_map/ppermute | solution.py:690
  16.1 12.3 %collective-permute-start.5 = (f32[1,768]{1,0:T(1,128)S(1)}, f32[1,768]{1,0:T(1,128)S(1)}, u32[]{:S(2)}, u32[]{:S(2)}) collective-permute-start(f32[1,768]{1,0:T(1,128)S(1)} %reshape.677), channel_id=1, source_target_pairs={{0,2},{1,3},{2,0},{3,1},{4,6},{5,7},{6,4},{7,5},{8,10},{9,11},{10,... | collective-permute-start | bytes 9224 | tf_op jit(solution)/shard_map/ppermute | solution.py:690
  25.4 13.3 %collective-permute-start.8 = (bf16[96,3072]{1,0:T(8,128)(2,1)S(1)}, bf16[96,3072]{1,0:T(8,128)(2,1)S(1)}, u32[]{:S(2)}, u32[]{:S(2)}) collective-permute-start(bf16[96,3072]{1,0:T(8,128)(2,1)S(1)} %pad_maximum_fusion.4), channel_id=1, source_target_pairs={{0,1},{1,0},{2,3},{3,2},{4,5},{5,4},{6,7},{7,6},{8,9},{9,8},{10,11... | collective-permute-start | bytes 1769480 | tf_op jit(solution)/shard_map/ppermute | solution.py:690
  28.4 13.6 %collective-permute-start.6 = (f32[1,1536]{1,0:T(1,128)S(1)}, f32[1,1536]{1,0:T(1,128)S(1)}, u32[]{:S(2)}, u32[]{:S(2)}) collective-permute-start(f32[1,1536]{1,0:T(1,128)S(1)} %pad_maximum_fusion.17), channel_id=1, source_target_pairs={{0,1},{1,0},{2,3},{3,2},{4,5},{5,4},{6,7},{7,6},{8,9},{9,8},{10,11... | collective-permute-start | bytes 18440 | tf_op jit(solution)/shard_map/ppermute | solution.py:690
  28.6 21.4 %collective-permute-start.2 = (bf16[96,2304]{1,0:T(8,128)(2,1)S(1)}, bf16[96,2304]{1,0:T(8,128)(2,1)}, u32[]{:S(2)}, u32[]{:S(2)}) collective-permute-start(bf16[96,2304]{1,0:T(8,128)(2,1)S(1)} %pad_maximum_fusion.8.refs_0_), channel_id=1, source_target_pairs={{0,8},{4,12},{8,0},{12,4},{16,24},{20,28},{24,16},{28,20},{1,9},{5... | collective-permute-start | bytes 1327112 | tf_op jit(solution)/shard_map/ppermute | solution.py:690
  29.8 20.1 %collective-permute-start.3 = (bf16[96,2304]{1,0:T(8,128)(2,1)S(1)}, bf16[96,2304]{1,0:T(8,128)(2,1)}, u32[]{:S(2)}, u32[]{:S(2)}) collective-permute-start(bf16[96,2304]{1,0:T(8,128)(2,1)S(1)} %pad_maximum_fusion.8.refs_0_), channel_id=1, source_target_pairs={{0,16},{4,20},{8,24},{12,28},{16,0},{20,4},{24,8},{28,12},{1,17},{... | collective-permute-start | bytes 1327112 | tf_op jit(solution)/shard_map/ppermute | solution.py:690
  30.9 19.0 %collective-permute-start.4 = (bf16[96,2304]{1,0:T(8,128)(2,1)S(1)}, bf16[96,2304]{1,0:T(8,128)(2,1)}, u32[]{:S(2)}, u32[]{:S(2)}) collective-permute-start(bf16[96,2304]{1,0:T(8,128)(2,1)S(1)} %pad_maximum_fusion.8.refs_0_), channel_id=1, source_target_pairs={{0,24},{4,28},{8,16},{12,20},{16,8},{20,12},{24,0},{28,4},{1,25},{... | collective-permute-start | bytes 1327112 | tf_op jit(solution)/shard_map/ppermute | solution.py:690
  38.8 21.0 %collective-permute-start.10 = (bf16[1,96,2304]{2,1,0:T(8,128)(2,1)S(1)}, bf16[1,96,2304]{2,1,0:T(8,128)(2,1)S(1)}, u32[]{:S(2)}, u32[]{:S(2)}) collective-permute-start(bf16[1,96,2304]{2,1,0:T(8,128)(2,1)S(1)} %get-tuple-element.261), channel_id=1, source_target_pairs={{0,16},{4,20},{8,24},{12,28},{16,0},{20,4},{24,8},{28,12},{1,17},{... | collective-permute-start | bytes 1327112 | tf_op jit(solution)/shard_map/ppermute | solution.py:690
  42.0 17.9 %collective-permute-start.9 = (bf16[1,96,2304]{2,1,0:T(8,128)(2,1)S(1)}, bf16[1,96,2304]{2,1,0:T(8,128)(2,1)S(1)}, u32[]{:S(2)}, u32[]{:S(2)}) collective-permute-start(bf16[1,96,2304]{2,1,0:T(8,128)(2,1)S(1)} %get-tuple-element.262), channel_id=1, source_target_pairs={{0,8},{4,12},{8,0},{12,4},{16,24},{20,28},{24,16},{28,20},{1,9},{5... | collective-permute-start | bytes 1327112 | tf_op jit(solution)/shard_map/ppermute | solution.py:690
  50.0 13.8 %collective-permute-start.13 = (bf16[96,2304]{1,0:T(8,128)(2,1)S(1)}, bf16[96,2304]{1,0:T(8,128)(2,1)S(1)}, u32[]{:S(2)}, u32[]{:S(2)}) collective-permute-start(bf16[96,2304]{1,0:T(8,128)(2,1)S(1)} %pad_maximum_fusion.8.refs_0_), channel_id=1, source_target_pairs={{0,4},{4,0},{8,12},{12,8},{16,20},{20,16},{24,28},{28,24},{1,5},{5... | collective-permute-start | bytes 1327112 | tf_op jit(solution)/shard_map/ppermute | solution.py:690
  60.0 26.9 %collective-permute-start.11 = (bf16[2,96,2304]{2,1,0:T(8,128)(2,1)S(1)}, bf16[2,96,2304]{2,1,0:T(8,128)(2,1)S(1)}, u32[]{:S(2)}, u32[]{:S(2)}) collective-permute-start(bf16[2,96,2304]{2,1,0:T(8,128)(2,1)S(1)} %pad_maximum_fusion.1.refs_0_), channel_id=1, source_target_pairs={{0,16},{4,20},{8,24},{12,28},{16,0},{20,4},{24,8},{28,12},{1,17},{... | collective-permute-start | bytes 2654216 | tf_op jit(solution)/shard_map/ppermute | solution.py:690
  60.4 26.5 %collective-permute-start.12 = (bf16[2,96,2304]{2,1,0:T(8,128)(2,1)S(1)}, bf16[2,96,2304]{2,1,0:T(8,128)(2,1)S(1)}, u32[]{:S(2)}, u32[]{:S(2)}) collective-permute-start(bf16[2,96,2304]{2,1,0:T(8,128)(2,1)S(1)} %pad_maximum_fusion.2.refs_2_), channel_id=1, source_target_pairs={{0,8},{4,12},{8,0},{12,4},{16,24},{20,28},{24,16},{28,20},{1,9},{5... | collective-permute-start | bytes 2654216 | tf_op jit(solution)/shard_map/ppermute | solution.py:690
  61.6 3.8 %collective-permute-start.14 = (bf16[96,2304]{1,0:T(8,128)(2,1)}, bf16[96,2304]{1,0:T(8,128)(2,1)S(1)}, u32[]{:S(2)}, u32[]{:S(2)}) collective-permute-start(bf16[96,2304]{1,0:T(8,128)(2,1)} %collective-permute-done.2.refs_1_), channel_id=1, source_target_pairs={{0,4},{4,0},{8,12},{12,8},{16,20},{20,16},{24,28},{28,24},{1,5},{5... | collective-permute-start | bytes 1327112 | tf_op jit(solution)/shard_map/ppermute | solution.py:690
  63.7 2.3 collective-permute-start.15
  63.7 3.2 collective-permute-start.16
  65.4 24.5 %collective-permute-start.17 = (bf16[2,96,2304]{2,1,0:T(8,128)(2,1)S(1)}, bf16[2,96,2304]{2,1,0:T(8,128)(2,1)}, u32[]{:S(2)}, u32[]{:S(2)}) collective-permute-start(bf16[2,96,2304]{2,1,0:T(8,128)(2,1)S(1)} %pad_maximum_fusion.1.refs_0_), channel_id=1, source_target_pairs={{0,4},{4,0},{8,12},{12,8},{16,20},{20,16},{24,28},{28,24},{1,5},{5... | collective-permute-start | bytes 2654216 | tf_op jit(solution)/shard_map/ppermute | solution.py:690
  66.1 23.8 %collective-permute-start.19 = (bf16[2,96,2304]{2,1,0:T(8,128)(2,1)S(1)}, bf16[2,96,2304]{2,1,0:T(8,128)(2,1)}, u32[]{:S(2)}, u32[]{:S(2)}) collective-permute-start(bf16[2,96,2304]{2,1,0:T(8,128)(2,1)S(1)} %pad_maximum_fusion.2.refs_2_), channel_id=1, source_target_pairs={{0,4},{4,0},{8,12},{12,8},{16,20},{20,16},{24,28},{28,24},{1,5},{5... | collective-permute-start | bytes 2654216 | tf_op jit(solution)/shard_map/ppermute | solution.py:690
  86.9 3.0 collective-permute-start.18
  87.4 3.5 %collective-permute-start.20 = (bf16[2,96,2304]{2,1,0:T(8,128)(2,1)S(1)}, bf16[2,96,2304]{2,1,0:T(8,128)(2,1)}, u32[]{:S(2)}, u32[]{:S(2)}) collective-permute-start(bf16[2,96,2304]{2,1,0:T(8,128)(2,1)S(1)} %collective-permute-done.12.refs_3_), channel_id=1, source_target_pairs={{0,4},{4,0},{8,12},{12,8},{16,20},{20,16},{24,28},{28,24},{1,5},{5... | collective-permute-start | bytes 2654216 | tf_op jit(solution)/shard_map/ppermute | solution.py:690
  113.8 2.8 collective-permute-start.21
  115.3 3.8 %collective-permute-start.22 = (bf16[8,768]{1,0:T(8,128)(2,1)}, bf16[8,768]{1,0:T(8,128)(2,1)S(1)}, u32[]{:S(2)}, u32[]{:S(2)}) collective-permute-start(bf16[8,768]{1,0:T(8,128)(2,1)} %get-tuple-element.148), channel_id=1, source_target_pairs={{0,2},{1,3},{2,0},{3,1},{4,6},{5,7},{6,4},{7,5},{8,10},{9,11},{10,... | collective-permute-start | bytes 36872 | tf_op jit(solution)/shard_map/ppermute | solution.py:690
  116.1 3.0 collective-permute-start.23
  120.5 5.4 %collective-permute-start.24 = (bf16[64,768]{1,0:T(8,128)(2,1)S(1)}, bf16[64,768]{1,0:T(8,128)(2,1)S(1)}, u32[]{:S(2)}, u32[]{:S(2)}) collective-permute-start(bf16[64,768]{1,0:T(8,128)(2,1)S(1)} %constant_dynamic-update-slice_fusion), channel_id=1, source_target_pairs={{0,8},{4,12},{8,0},{12,4},{16,24},{20,28},{24,16},{28,20},{1,9},{5... | collective-permute-start | bytes 294920 | tf_op jit(solution)/shard_map/ppermute | solution.py:690
  121.6 6.2 %collective-permute-start.25 = (bf16[64,768]{1,0:T(8,128)(2,1)S(1)}, bf16[64,768]{1,0:T(8,128)(2,1)S(1)}, u32[]{:S(2)}, u32[]{:S(2)}) collective-permute-start(bf16[64,768]{1,0:T(8,128)(2,1)S(1)} %constant_dynamic-update-slice_fusion), channel_id=1, source_target_pairs={{0,16},{4,20},{8,24},{12,28},{16,0},{20,4},{24,8},{28,12},{1,17},{... | collective-permute-start | bytes 294920 | tf_op jit(solution)/shard_map/ppermute | solution.py:690
  122.1 6.7 %collective-permute-start.26 = (bf16[64,768]{1,0:T(8,128)(2,1)S(1)}, bf16[64,768]{1,0:T(8,128)(2,1)S(1)}, u32[]{:S(2)}, u32[]{:S(2)}) collective-permute-start(bf16[64,768]{1,0:T(8,128)(2,1)S(1)} %constant_dynamic-update-slice_fusion), channel_id=1, source_target_pairs={{0,24},{4,28},{8,16},{12,20},{16,8},{20,12},{24,0},{28,4},{1,25},{... | collective-permute-start | bytes 294920 | tf_op jit(solution)/shard_map/ppermute | solution.py:690
  123.3 6.5 %collective-permute-start.27 = (bf16[64,768]{1,0:T(8,128)(2,1)S(1)}, bf16[64,768]{1,0:T(8,128)(2,1)S(1)}, u32[]{:S(2)}, u32[]{:S(2)}) collective-permute-start(bf16[64,768]{1,0:T(8,128)(2,1)S(1)} %constant_dynamic-update-slice_fusion), channel_id=1, source_target_pairs={{0,4},{4,0},{8,12},{12,8},{16,20},{20,16},{24,28},{28,24},{1,5},{5... | collective-permute-start | bytes 294920 | tf_op jit(solution)/shard_map/ppermute | solution.py:690
  125.8 4.0 %collective-permute-start.28 = (bf16[64,768]{1,0:T(8,128)(2,1)S(1)}, bf16[64,768]{1,0:T(8,128)(2,1)S(1)}, u32[]{:S(2)}, u32[]{:S(2)}) collective-permute-start(bf16[64,768]{1,0:T(8,128)(2,1)S(1)} %collective-permute-done.24), channel_id=1, source_target_pairs={{0,4},{4,0},{8,12},{12,8},{16,20},{20,16},{24,28},{28,24},{1,5},{5... | collective-permute-start | bytes 294920 | tf_op jit(solution)/shard_map/ppermute | solution.py:690
  127.8 2.0 collective-permute-start.29
  128.7 2.0 collective-permute-start.30
  173.8 5.4 %collective-permute-start.32 = (bf16[2,4,96,768]{3,2,1,0:T(8,128)(2,1)}, bf16[2,4,96,768]{3,2,1,0:T(8,128)(2,1)S(1)}, u32[]{:S(2)}, u32[]{:S(2)}) collective-permute-start(bf16[2,4,96,768]{3,2,1,0:T(8,128)(2,1)} %get-tuple-element.157), channel_id=1, source_target_pairs={{0,4},{4,0},{8,12},{12,8},{16,20},{20,16},{24,28},{28,24},{1,5},{5... | collective-permute-start | bytes 3538952 | tf_op jit(solution)/shard_map/ppermute | solution.py:690
  174.2 6.7 %collective-permute-start.31 = (bf16[2,4,96,768]{3,2,1,0:T(8,128)(2,1)}, bf16[2,4,96,768]{3,2,1,0:T(8,128)(2,1)S(1)}, u32[]{:S(2)}, u32[]{:S(2)}) collective-permute-start(bf16[2,4,96,768]{3,2,1,0:T(8,128)(2,1)} %get-tuple-element.155), channel_id=1, source_target_pairs={{0,4},{4,0},{8,12},{12,8},{16,20},{20,16},{24,28},{28,24},{1,5},{5... | collective-permute-start | bytes 3538952 | tf_op jit(solution)/shard_map/ppermute | solution.py:690
  175.8 2.6 collective-permute-start.33
  182.5 28.5 %collective-permute-start.36 = (bf16[2,4,96,768]{3,2,1,0:T(8,128)(2,1)}, bf16[2,4,96,768]{3,2,1,0:T(8,128)(2,1)}, u32[]{:S(2)}, u32[]{:S(2)}) collective-permute-start(bf16[2,4,96,768]{3,2,1,0:T(8,128)(2,1)} %get-tuple-element.167), channel_id=1, source_target_pairs={{0,4},{4,0},{8,12},{12,8},{16,20},{20,16},{24,28},{28,24},{1,5},{5... | collective-permute-start | bytes 3538952 | tf_op jit(solution)/shard_map/ppermute | solution.py:690
  182.9 28.1 %collective-permute-start.37 = (bf16[2,4,96,768]{3,2,1,0:T(8,128)(2,1)}, bf16[2,4,96,768]{3,2,1,0:T(8,128)(2,1)}, u32[]{:S(2)}, u32[]{:S(2)}) collective-permute-start(bf16[2,4,96,768]{3,2,1,0:T(8,128)(2,1)} %get-tuple-element.168), channel_id=1, source_target_pairs={{0,4},{4,0},{8,12},{12,8},{16,20},{20,16},{24,28},{28,24},{1,5},{5... | collective-permute-start | bytes 3538952 | tf_op jit(solution)/shard_map/ppermute | solution.py:690
  183.0 28.0 %collective-permute-start.34 = (bf16[2,4,96,768]{3,2,1,0:T(8,128)(2,1)}, bf16[2,4,96,768]{3,2,1,0:T(8,128)(2,1)}, u32[]{:S(2)}, u32[]{:S(2)}) collective-permute-start(bf16[2,4,96,768]{3,2,1,0:T(8,128)(2,1)} %fusion.1), channel_id=1, source_target_pairs={{0,8},{4,12},{8,0},{12,4},{16,24},{20,28},{24,16},{28,20},{1,9},{5... | collective-permute-start | bytes 3538952 | tf_op jit(solution)/shard_map/ppermute | solution.py:690
  183.8 27.2 %collective-permute-start.35 = (bf16[2,4,96,768]{3,2,1,0:T(8,128)(2,1)S(1)}, bf16[2,4,96,768]{3,2,1,0:T(8,128)(2,1)}, u32[]{:S(2)}, u32[]{:S(2)}) collective-permute-start(bf16[2,4,96,768]{3,2,1,0:T(8,128)(2,1)S(1)} %fusion), channel_id=1, source_target_pairs={{0,16},{4,20},{8,24},{12,28},{16,0},{20,4},{24,8},{28,12},{1,17},{... | collective-permute-start | bytes 3538952 | tf_op jit(solution)/shard_map/ppermute | solution.py:690
  184.8 26.2 %collective-permute-start.38 = (f32[6,768]{1,0:T(8,128)S(1)}, f32[6,768]{1,0:T(8,128)S(1)}, u32[]{:S(2)}, u32[]{:S(2)}) collective-permute-start(f32[6,768]{1,0:T(8,128)S(1)} %pad_maximum_fusion.13), channel_id=1, source_target_pairs={{0,1},{1,0},{2,3},{3,2},{4,5},{5,4},{6,7},{7,6},{8,9},{9,8},{10,11... | collective-permute-start | bytes 55304 | tf_op jit(solution)/shard_map/ppermute | solution.py:690
  215.6 21.8 %collective-permute-start.40 = (bf16[1,4,96,768]{3,2,1,0:T(8,128)(2,1)}, bf16[1,4,96,768]{3,2,1,0:T(8,128)(2,1)S(1)}, u32[]{:S(2)}, u32[]{:S(2)}) collective-permute-start(bf16[1,4,96,768]{3,2,1,0:T(8,128)(2,1)} %fusion.13), channel_id=1, source_target_pairs={{0,16},{4,20},{8,24},{12,28},{16,0},{20,4},{24,8},{28,12},{1,17},{... | collective-permute-start | bytes 1769480 | tf_op jit(solution)/shard_map/ppermute | solution.py:690
  216.3 21.1 %collective-permute-start.41 = (bf16[1,4,96,768]{3,2,1,0:T(8,128)(2,1)}, bf16[1,4,96,768]{3,2,1,0:T(8,128)(2,1)S(1)}, u32[]{:S(2)}, u32[]{:S(2)}) collective-permute-start(bf16[1,4,96,768]{3,2,1,0:T(8,128)(2,1)} %fusion.17), channel_id=1, source_target_pairs={{0,8},{4,12},{8,0},{12,4},{16,24},{20,28},{24,16},{28,20},{1,9},{5... | collective-permute-start | bytes 1769480 | tf_op jit(solution)/shard_map/ppermute | solution.py:690
  217.2 20.2 %collective-permute-start.42 = (bf16[8,32,768]{2,1,0:T(8,128)(2,1)}, bf16[8,32,768]{2,1,0:T(8,128)(2,1)S(1)}, u32[]{:S(2)}, u32[]{:S(2)}) collective-permute-start(bf16[8,32,768]{2,1,0:T(8,128)(2,1)} %get-tuple-element.199), channel_id=1, source_target_pairs={{0,1},{1,0},{2,3},{3,2},{4,5},{5,4},{6,7},{7,6},{8,9},{9,8},{10,11... | collective-permute-start | bytes 1179656 | tf_op jit(solution)/shard_map/ppermute | solution.py:690
  220.6 16.8 %collective-permute-start.43 = (bf16[8,32,768]{2,1,0:T(8,128)(2,1)}, bf16[8,32,768]{2,1,0:T(8,128)(2,1)}, u32[]{:S(2)}, u32[]{:S(2)}) collective-permute-start(bf16[8,32,768]{2,1,0:T(8,128)(2,1)} %get-tuple-element.200), channel_id=1, source_target_pairs={{0,2},{1,3},{2,0},{3,1},{4,6},{5,7},{6,4},{7,5},{8,10},{9,11},{10,... | collective-permute-start | bytes 1179656 | tf_op jit(solution)/shard_map/ppermute | solution.py:690
  220.8 16.6 %collective-permute-start.39 = (f32[5,768]{1,0:T(8,128)S(1)}, f32[5,768]{1,0:T(8,128)S(1)}, u32[]{:S(2)}, u32[]{:S(2)}) collective-permute-start(f32[5,768]{1,0:T(8,128)S(1)} %pad_maximum_fusion.14), channel_id=1, source_target_pairs={{0,2},{1,3},{2,0},{3,1},{4,6},{5,7},{6,4},{7,5},{8,10},{9,11},{10,... | collective-permute-start | bytes 46088 | tf_op jit(solution)/shard_map/ppermute | solution.py:690
  237.4 7.1 %collective-permute-start.44 = (bf16[4,4,96,768]{3,2,1,0:T(8,128)(2,1)}, bf16[4,4,96,768]{3,2,1,0:T(8,128)(2,1)S(1)}, u32[]{:S(2)}, u32[]{:S(2)}) collective-permute-start(bf16[4,4,96,768]{3,2,1,0:T(8,128)(2,1)} %get-tuple-element.204), channel_id=1, source_target_pairs={{0,4},{4,0},{8,12},{12,8},{16,20},{20,16},{24,28},{28,24},{1,5},{5... | collective-permute-start | bytes 7077896 | tf_op jit(solution)/shard_map/ppermute | solution.py:690
  245.5 16.4 %collective-permute-start.48 = (bf16[2,96,1536]{2,1,0:T(8,128)(2,1)S(1)}, bf16[2,96,1536]{2,1,0:T(8,128)(2,1)S(1)}, u32[]{:S(2)}, u32[]{:S(2)}) collective-permute-start(bf16[2,96,1536]{2,1,0:T(8,128)(2,1)S(1)} %get-tuple-element.211), channel_id=1, source_target_pairs={{0,1},{1,0},{2,3},{3,2},{4,5},{5,4},{6,7},{7,6},{8,9},{9,8},{10,11... | collective-permute-start | bytes 1769480 | tf_op jit(solution)/shard_map/ppermute | solution.py:690
  248.2 27.8 %collective-permute-start.45 = (bf16[4,96,768]{2,1,0:T(8,128)(2,1)S(1)}, bf16[4,96,768]{2,1,0:T(8,128)(2,1)S(1)}, u32[]{:S(2)}, u32[]{:S(2)}) collective-permute-start(bf16[4,96,768]{2,1,0:T(8,128)(2,1)S(1)} %get-tuple-element.208), channel_id=1, source_target_pairs={{0,8},{4,12},{8,0},{12,4},{16,24},{20,28},{24,16},{28,20},{1,9},{5... | collective-permute-start | bytes 1769480 | tf_op jit(solution)/shard_map/ppermute | solution.py:690
  248.8 27.2 %collective-permute-start.46 = (bf16[4,96,768]{2,1,0:T(8,128)(2,1)S(1)}, bf16[4,96,768]{2,1,0:T(8,128)(2,1)S(1)}, u32[]{:S(2)}, u32[]{:S(2)}) collective-permute-start(bf16[4,96,768]{2,1,0:T(8,128)(2,1)S(1)} %get-tuple-element.209), channel_id=1, source_target_pairs={{0,16},{4,20},{8,24},{12,28},{16,0},{20,4},{24,8},{28,12},{1,17},{... | collective-permute-start | bytes 1769480 | tf_op jit(solution)/shard_map/ppermute | solution.py:690
  249.4 26.6 %collective-permute-start.47 = (bf16[4,96,768]{2,1,0:T(8,128)(2,1)S(1)}, bf16[4,96,768]{2,1,0:T(8,128)(2,1)S(1)}, u32[]{:S(2)}, u32[]{:S(2)}) collective-permute-start(bf16[4,96,768]{2,1,0:T(8,128)(2,1)S(1)} %get-tuple-element.210), channel_id=1, source_target_pairs={{0,24},{4,28},{8,16},{12,20},{16,8},{20,12},{24,0},{28,4},{1,25},{... | collective-permute-start | bytes 1769480 | tf_op jit(solution)/shard_map/ppermute | solution.py:690
  262.0 14.5 %collective-permute-start.49 = (bf16[1,96,1536]{2,1,0:T(8,128)(2,1)S(1)}, bf16[1,96,1536]{2,1,0:T(8,128)(2,1)S(1)}, u32[]{:S(2)}, u32[]{:S(2)}) collective-permute-start(bf16[1,96,1536]{2,1,0:T(8,128)(2,1)S(1)} %fusion.24), channel_id=1, source_target_pairs={{0,2},{1,3},{2,0},{3,1},{4,6},{5,7},{6,4},{7,5},{8,10},{9,11},{10,... | collective-permute-start | bytes 884744 | tf_op jit(solution)/shard_map/ppermute | solution.py:690
  263.5 12.5 %collective-permute-start.50 = (f32[5,768]{1,0:T(8,128)S(1)}, f32[5,768]{1,0:T(8,128)S(1)}, u32[]{:S(2)}, u32[]{:S(2)}) collective-permute-start(f32[5,768]{1,0:T(8,128)S(1)} %pad_maximum_fusion.15), channel_id=1, source_target_pairs={{0,8},{4,12},{8,0},{12,4},{16,24},{20,28},{24,16},{28,20},{1,9},{5... | collective-permute-start | bytes 46088 | tf_op jit(solution)/shard_map/ppermute | solution.py:690
  277.0 9.9 %collective-permute-start.51 = (bf16[2,96,768]{2,1,0:T(8,128)(2,1)S(1)}, bf16[2,96,768]{2,1,0:T(8,128)(2,1)S(1)}, u32[]{:S(2)}, u32[]{:S(2)}) collective-permute-start(bf16[2,96,768]{2,1,0:T(8,128)(2,1)S(1)} %get-tuple-element.219), channel_id=1, source_target_pairs={{0,1},{1,0},{2,3},{3,2},{4,5},{5,4},{6,7},{7,6},{8,9},{9,8},{10,11... | collective-permute-start | bytes 884744 | tf_op jit(solution)/shard_map/ppermute | solution.py:690
  280.0 16.1 %collective-permute-start.54 = (bf16[96,1536]{1,0:T(8,128)(2,1)S(1)}, bf16[96,1536]{1,0:T(8,128)(2,1)S(1)}, u32[]{:S(2)}, u32[]{:S(2)}) collective-permute-start(bf16[96,1536]{1,0:T(8,128)(2,1)S(1)} %fusion.25), channel_id=1, source_target_pairs={{0,8},{4,12},{8,0},{12,4},{16,24},{20,28},{24,16},{28,20},{1,9},{5... | collective-permute-start | bytes 884744 | tf_op jit(solution)/shard_map/ppermute | solution.py:690
  280.6 15.5 %collective-permute-start.55 = (bf16[96,1536]{1,0:T(8,128)(2,1)S(1)}, bf16[96,1536]{1,0:T(8,128)(2,1)S(1)}, u32[]{:S(2)}, u32[]{:S(2)}) collective-permute-start(bf16[96,1536]{1,0:T(8,128)(2,1)S(1)} %fusion.25), channel_id=1, source_target_pairs={{0,16},{4,20},{8,24},{12,28},{16,0},{20,4},{24,8},{28,12},{1,17},{... | collective-permute-start | bytes 884744 | tf_op jit(solution)/shard_map/ppermute | solution.py:690
  281.2 14.9 %collective-permute-start.56 = (bf16[96,1536]{1,0:T(8,128)(2,1)S(1)}, bf16[96,1536]{1,0:T(8,128)(2,1)S(1)}, u32[]{:S(2)}, u32[]{:S(2)}) collective-permute-start(bf16[96,1536]{1,0:T(8,128)(2,1)S(1)} %fusion.25), channel_id=1, source_target_pairs={{0,24},{4,28},{8,16},{12,20},{16,8},{20,12},{24,0},{28,4},{1,25},{... | collective-permute-start | bytes 884744 | tf_op jit(solution)/shard_map/ppermute | solution.py:690
  287.0 9.1 %collective-permute-start.52 = (bf16[1,96,768]{2,1,0:T(8,128)(2,1)S(1)}, bf16[1,96,768]{2,1,0:T(8,128)(2,1)S(1)}, u32[]{:S(2)}, u32[]{:S(2)}) collective-permute-start(bf16[1,96,768]{2,1,0:T(8,128)(2,1)S(1)} %fusion.27), channel_id=1, source_target_pairs={{0,2},{1,3},{2,0},{3,1},{4,6},{5,7},{6,4},{7,5},{8,10},{9,11},{10,... | collective-permute-start | bytes 442376 | tf_op jit(solution)/shard_map/ppermute | solution.py:690
  288.3 7.7 %collective-permute-start.53 = (f32[5,768]{1,0:T(8,128)S(1)}, f32[5,768]{1,0:T(8,128)S(1)}, u32[]{:S(2)}, u32[]{:S(2)}) collective-permute-start(f32[5,768]{1,0:T(8,128)S(1)} %add.389), channel_id=1, source_target_pairs={{0,16},{4,20},{8,24},{12,28},{16,0},{20,4},{24,8},{28,12},{1,17},{... | collective-permute-start | bytes 46088 | tf_op jit(solution)/shard_map/ppermute | solution.py:690
  296.4 4.2 %collective-permute-start.57 = (bf16[4,96,1536]{2,1,0:T(8,128)(2,1)S(1)}, bf16[4,96,1536]{2,1,0:T(8,128)(2,1)S(1)}, u32[]{:S(2)}, u32[]{:S(2)}) collective-permute-start(bf16[4,96,1536]{2,1,0:T(8,128)(2,1)S(1)} %pad_maximum_fusion.near), channel_id=1, source_target_pairs={{0,4},{4,0},{8,12},{12,8},{16,20},{20,16},{24,28},{28,24},{1,5},{5... | collective-permute-start | bytes 3538952 | tf_op jit(solution)/shard_map/ppermute | solution.py:690
  297.2 18.3 %collective-permute-start.58 = (bf16[8,32,768]{2,1,0:T(8,128)(2,1)S(1)}, bf16[8,32,768]{2,1,0:T(8,128)(2,1)S(1)}, u32[]{:S(2)}, u32[]{:S(2)}) collective-permute-start(bf16[8,32,768]{2,1,0:T(8,128)(2,1)S(1)} %copy-done.35), channel_id=1, source_target_pairs={{0,3},{1,2},{2,1},{3,0},{4,7},{5,6},{6,5},{7,4},{8,11},{9,10},{10,... | collective-permute-start | bytes 1179656 | tf_op jit(solution)/shard_map/ppermute | solution.py:690
  297.9 17.6 %collective-permute-start.59 = (bf16[96,768]{1,0:T(8,128)(2,1)S(1)}, bf16[96,768]{1,0:T(8,128)(2,1)S(1)}, u32[]{:S(2)}, u32[]{:S(2)}) collective-permute-start(bf16[96,768]{1,0:T(8,128)(2,1)S(1)} %fusion.28), channel_id=1, source_target_pairs={{0,8},{4,12},{8,0},{12,4},{16,24},{20,28},{24,16},{28,20},{1,9},{5... | collective-permute-start | bytes 442376 | tf_op jit(solution)/shard_map/ppermute | solution.py:690
  298.7 16.8 %collective-permute-start.60 = (bf16[96,768]{1,0:T(8,128)(2,1)S(1)}, bf16[96,768]{1,0:T(8,128)(2,1)S(1)}, u32[]{:S(2)}, u32[]{:S(2)}) collective-permute-start(bf16[96,768]{1,0:T(8,128)(2,1)S(1)} %fusion.28), channel_id=1, source_target_pairs={{0,16},{4,20},{8,24},{12,28},{16,0},{20,4},{24,8},{28,12},{1,17},{... | collective-permute-start | bytes 442376 | tf_op jit(solution)/shard_map/ppermute | solution.py:690
  299.4 16.1 %collective-permute-start.61 = (bf16[96,768]{1,0:T(8,128)(2,1)S(1)}, bf16[96,768]{1,0:T(8,128)(2,1)S(1)}, u32[]{:S(2)}, u32[]{:S(2)}) collective-permute-start(bf16[96,768]{1,0:T(8,128)(2,1)S(1)} %fusion.28), channel_id=1, source_target_pairs={{0,24},{4,28},{8,16},{12,20},{16,8},{20,12},{24,0},{28,4},{1,25},{... | collective-permute-start | bytes 442376 | tf_op jit(solution)/shard_map/ppermute | solution.py:690
  315.7 6.9 %collective-permute-start.62 = (bf16[4,96,768]{2,1,0:T(8,128)(2,1)S(1)}, bf16[4,96,768]{2,1,0:T(8,128)(2,1)S(1)}, u32[]{:S(2)}, u32[]{:S(2)}) collective-permute-start(bf16[4,96,768]{2,1,0:T(8,128)(2,1)S(1)} %pad_maximum_fusion.5.near), channel_id=1, source_target_pairs={{0,4},{4,0},{8,12},{12,8},{16,20},{20,16},{24,28},{28,24},{1,5},{5... | collective-permute-start | bytes 1769480 | tf_op jit(solution)/shard_map/ppermute | solution.py:690
  (35 other events, 308.2 us)
where the time goes:
time: 331 us; the launch traced here: 328 us
  Pallas kernels  133 us (40%)
  waiting for transfers between devices  84.7 us (26%)
  starting transfers between devices  71 us (21%)
  local copies, waits for them, and re-layouts  19.8 us (6%)
  other arithmetic  16.7 us (5%)
    ppermute x63, waiting for transfers between devices, swap(): lax.ppermute(value, axis, [(i, i ^ mask) for i in range(lax.axis_size(axi...  84.7 us
    ppermute x63, starting transfers between devices, swap(): lax.ppermute(value, axis, [(i, i ^ mask) for i in range(lax.axis_size(axi...  71 us
    pallas_call x1, Pallas kernels, shards(): call(ffn_backward, (send_shape, half_shape, half_shape) * 2 + (shape((row...  41.1 us
    pallas_call x1, Pallas kernels, shards(): call(ffn_forward, (act_shape, act_shape, shape((rows, width), F32), shape...  22.9 us
    pallas_call x1, Pallas kernels, shards(): pl.pallas_call(attention_backward, out_shape=(shape((pad, 3 * width), LOW...  21.4 us
    pallas_call x1, Pallas kernels, shards(): pl.pallas_call(attention_forward, out_shape=(shape((pad, 3 * width), LOW)...  19.1 us
    pallas_call x1, Pallas kernels, shards(): pl.pallas_call(attention_weights, out_shape=(shape((chips, t_count, slab,...  9.77 us
    pallas_call x2, Pallas kernels, finish(): pl.pallas_call(kernel, out_shape=tuple((shape(dims, F32) for dims in outs...  8.96 us
  transfers between devices with their start and end apart: 63, of which 18 were waited for; matrix products, arithmetic and copies ran while one was open for 6% of the time, Pallas kernels for 20%

commit v1 on v0

--- a/solution.py
+++ b/solution.py
@@ -791,30 +791,30 @@
 
     attn_piece = jnp.concatenate([by_part(rows_piece(w_qkv)), columns_piece(w_out)], axis=1)
     attn_piece, up_early, down_early = tie(attn_piece, up_weight, down_weight)
-    line_bits = bits_of(t_count)[::-1]
+    near_bits = bits_of(t_count)
+    line_bits = near_bits[::-1]
 
     def widen_line(parts, bit):
         return parts + [swap(jnp.concatenate(parts, axis=1), bit, "tensor")]
 
-    def line_order():
+    def line_order(bits):
         order = [0]
-        for bit in line_bits:
+        for bit in bits:
             order += [item ^ bit for item in order]
         return order
 
-    def by_distance(parts, columns):
+    def by_distance(parts, columns, bits):
         wide = jnp.concatenate(parts, axis=1)
-        order = line_order()
+        order = line_order(bits)
         return [wide[:, order.index(d) * columns : (order.index(d) + 1) * columns] for d in range(t_count)]
 
     attn_parts = widen_line([attn_piece], line_bits[0])
     ffn_piece = jnp.concatenate([rows_piece(up_early), columns_piece(down_early)], axis=1)
-    attn_parts[1], ffn_piece, up_projection_bias = tie(attn_parts[1], ffn_piece, up_projection_bias)
     for bit in line_bits[1:]:
         attn_parts = widen_line(attn_parts, bit)
-    ffn_parts = widen_line([ffn_piece], line_bits[0])
-    bias_parts = widen_line([up_projection_bias.reshape(1, units)], line_bits[0])
-    attn_line = jnp.concatenate(by_distance(attn_parts, block)[1:], axis=1)
+    ffn_parts = widen_line([ffn_piece], near_bits[0])
+    bias_parts = widen_line([up_projection_bias.reshape(1, units)], near_bits[0])
+    attn_line = jnp.concatenate(by_distance(attn_parts, block, line_bits)[1:], axis=1)
 
     order = np.arange(sentences)
     ahead = (lengths[None, :] > lengths[:, None]) | (
@@ -868,13 +868,14 @@
     )(table, chosen, tokens)
 
     attn_chips = gather_chips(attn_line)
-    for bit in line_bits[1:]:
+    for bit in near_bits[1:]:
         ffn_parts = widen_line(ffn_parts, bit)
         bias_parts = widen_line(bias_parts, bit)
-    bias_all = jnp.stack(by_distance(bias_parts, units))
+    ffn_parts[-1], bias_parts[-1], packed = tie(ffn_parts[-1], bias_parts[-1], packed)
+    bias_all = jnp.stack(by_distance(bias_parts, units, near_bits))
     *attn_chips, packed = tie(*attn_chips, packed)
     attn_pieces = gather_cores(attn_chips)
-    ffn_line = jnp.concatenate(by_distance(ffn_parts, 2 * units)[1:], axis=1)
+    ffn_line = jnp.concatenate(by_distance(ffn_parts, 2 * units, near_bits)[1:], axis=1)
     middle = ffn_line.shape[1] // 2
     plane_bits = bits_of(chips)
     spread, orders = [], []
@@ -1046,7 +1047,6 @@
     high = chip_bits[-1]
     down_early, up_early = swap(down_early, 1), swap(up_early, 1)
     small = jnp.concatenate([bias_sum.reshape(t_count, units), sums])
-    small = small + swap(small, 1)
     down_sent, up_sent, small, attn_low = tie(
         add(pick(down_mine, 1, 1), down_early).astype(LOW),
         add(pick(up_mine, 1, high), up_early).astype(LOW),
@@ -1094,7 +1094,6 @@
     norms, small_got, bias_part = small_step(norms, bias_part, 2)
     down_got, up_got = swap(down_sent, 2 * high), swap(up_sent, 2)
     input_landed = [input_blocks[0]] + [None] * (t_count - 1)
-    input_landed[2] = swap(input_blocks[2], 2, "tensor")
     input_landed[1] = swap(input_blocks[1], 1, "tensor")
 
     attn_mine, attn_other = pl.pallas_call(
@@ -1132,8 +1131,8 @@
             name=kernel.__name__,
         )(table, near, far)
 
-    attn_other, small_got, down_got, up_got, input_landed[1], input_landed[2] = tie(
-        attn_other, small_got, down_got, up_got, input_landed[1], input_landed[2]
+    attn_other, small_got, down_got, up_got, input_landed[1] = tie(
+        attn_other, small_got, down_got, up_got, input_landed[1]
     )
     norms, bias_part = small_sum(norms, small_got, bias_part)
     small = jnp.concatenate([bias_part, norms])
@@ -1143,19 +1142,20 @@
         [add(*kept(up_terms, 1, up_got))[0], add(*kept(down_terms, 1, down_got))[0]], axis=2
     )
     ffn_line = [ffn_line.astype(LOW)]
-    ffn_sent, small, *attn_sent = tie(sent(ffn_line, 1), small, *attn_sent)
+    ffn_sent, input_blocks[2], *attn_sent = tie(
+        sent(ffn_line, 1), input_blocks[2], *attn_sent
+    )
     attn_got = [attn_got[0]] + [swap(item, 2 * m) for m, item in zip(range(1, chips), attn_sent)]
     ffn_got = swap(ffn_sent, 1, "tensor")
-    small_got = swap(small, 2)
+    input_landed[2] = swap(input_blocks[2], 2, "tensor")
 
     ffn_line = kept(ffn_line, 1, ffn_got)
     ffn_got = swap(sent(ffn_line, 1), 2, "tensor")
-    *attn_got, ffn_got, small_got = tie(*attn_got, ffn_got, small_got)
-    small = small + small_got
+    *attn_got, ffn_got, small, input_landed[2] = tie(*attn_got, ffn_got, small, input_landed[2])
     attn_line = [add(attn_mine[0], *attn_got).astype(LOW)]
     ffn_sum = add(*kept(ffn_line, 1, ffn_got))[0].astype(LOW)
     attn_sent, ffn_sum, small = tie(sent(attn_line, 1), ffn_sum, small)
-    small_got = swap(small, 4)
+    small_got = swap(small, 2)
     attn_got = swap(attn_sent, 1, "tensor")
     ffn_chips = gather_chips(ffn_sum)
     attn_line = kept(attn_line, 1, attn_got)
@@ -1171,7 +1171,12 @@
     attn_chips = gather_chips(attn_sum)
     input_landed[3] = swap(input_blocks[3], 3, "tensor")
     up_grad, down_grad = finish(place_grads, ffn_chips, ((width, units), (units, width)), units)
-    attn_chips[0], up_grad, input_landed[3] = tie(attn_chips[0], up_grad, input_landed[3])
+    small_got = swap(small, 4)
+    attn_chips[0], up_grad, input_landed[3], small_got = tie(
+        attn_chips[0], up_grad, input_landed[3], small_got
+    )
+    small = small + small_got
+    small_got = swap(small, 1)
     qkv_grad, out_grad = finish(
         place_attention_grads, attn_chips, ((3 * ctx_cols, width), (ctx_cols, width)), block
     )
@@ -1184,6 +1189,7 @@
         cost_estimate=cost(0, 4 * share * sentences * width),
         name="send_home",
     )(jnp.tile(source, STEP).reshape(-1, 1), *input_landed)
+    small = small + small_got
     bias_sum, norms = small[0], small[1:]
     return (
         returned,

time: 331 us -> 327 us (0.988)
  transfers between devices with their start and end apart: 63 -> 63, of which waited for: 18 -> 19; matrix products, arithmetic and copies ran while one was open for 6% -> 5% of each run, Pallas kernels for 20% -> 20%
where the time goes in v1:
time: 327 us; the launch traced here: 323 us
  Pallas kernels  133 us (41%)
  waiting for transfers between devices  82.6 us (25%)
  starting transfers between devices  70 us (21%)
  local copies, waits for them, and re-layouts  19 us (6%)
  other arithmetic  16 us (5%)
    ppermute x63, waiting for transfers between devices, swap(): lax.ppermute(value, axis, [(i, i ^ mask) for i in range(lax.axis_size(axi...  82.6 us
    ppermute x63, starting transfers between devices, swap(): lax.ppermute(value, axis, [(i, i ^ mask) for i in range(lax.axis_size(axi...  70 us
    pallas_call x1, Pallas kernels, shards(): call(ffn_backward, (send_shape, half_shape, half_shape) * 2 + (shape((row...  41.1 us
    pallas_call x1, Pallas kernels, shards(): call(ffn_forward, (act_shape, act_shape, shape((rows, width), F32), shape...  23 us
    pallas_call x1, Pallas kernels, shards(): pl.pallas_call(attention_backward, out_shape=(shape((pad, 3 * width), LOW...  21.4 us
    pallas_call x1, Pallas kernels, shards(): pl.pallas_call(attention_forward, out_shape=(shape((pad, 3 * width), LOW)...  19.1 us
    pallas_call x1, Pallas kernels, shards(): pl.pallas_call(attention_weights, out_shape=(shape((chips, t_count, slab,...  9.77 us
    pallas_call x2, Pallas kernels, finish(): pl.pallas_call(kernel, out_shape=tuple((shape(dims, F32) for dims in outs...  8.96 us
  transfers between devices with their start and end apart: 63, of which 19 were waited for; matrix products, arithmetic and copies ran while one was open for 5% of the time, Pallas kernels for 20%

profile of v1, /device:TPU:9, one launch (start us, length us, event | category | flops | bytes accessed | tf_op | source)
XLA Modules:
  0.0 323.2 jit_solution(4016907578279908683)
XLA Ops:
  0.7 1.2 constant_dynamic-slice_fusion.2
  2.0 1.0 constant_dynamic-slice_fusion.1
  3.2 2.4 collective-permute-start
  7.5 1.3 collective-permute-start.7
  12.9 2.7 collective-permute-done.5
  15.6 2.6 collective-permute-start.6
  18.2 6.4 %collective-permute-done.1 = bf16[96,1536]{1,0:T(8,128)(2,1)S(1)} collective-permute-done((bf16[96,1536]{1,0:T(8,128)(2,1)S(1)}, bf16[96,1536]{1,0:T(8,128)(2,1)S(1)}, u32[]{:S(2)}, u32[]{:S(2)}) %collective-permute-start.1) | collective-permute-done | bytes 294944 | tf_op jit(solution)/shard_map/ppermute | solution.py:690
  24.8 1.3 collective-permute-start.2
  26.0 1.1 collective-permute-start.3
  27.5 6.2 %pack.1 = (bf16[1152,768]{1,0:T(8,128)(2,1)}, bf16[8,96,1024]{2,1,0:T(8,128)(2,1)}) custom-call(s32[88]{0:T(128)} %concatenate.62.table, s32[8]{0:T(128)} %copy-done.32, bf16[128,32,768]{2,1,0:T(8,128)(2,1)} %tokens.1), custom_call_target="tpu_custom_call" | custom-call | bytes 6 | tf_op jit(solution)/shard_map/pack/pallas_call | solution.py:859
  33.7 7.6 %collective-permute-done.8 = f32[1,1536]{1,0:T(1,128)S(1)} collective-permute-done((f32[1,1536]{1,0:T(1,128)S(1)}, f32[1,1536]{1,0:T(1,128)S(1)}, u32[]{:S(2)}, u32[]{:S(2)}) %collective-permute-start.8) | collective-permute-done | bytes 6176 | tf_op jit(solution)/shard_map/ppermute | solution.py:690
  41.4 1.3 collective-permute-start.10
  43.5 2.4 collective-permute-done.4.refs_3_
  45.9 3.8 %collective-permute-start.13 = (bf16[96,2304]{1,0:T(8,128)(2,1)S(1)}, bf16[96,2304]{1,0:T(8,128)(2,1)S(1)}, u32[]{:S(2)}, u32[]{:S(2)}) collective-permute-start(bf16[96,2304]{1,0:T(8,128)(2,1)S(1)} %pad_maximum_fusion.7.refs_0_), channel_id=1, source_target_pairs={{0,4},{4,0},{8,12},{12,8},{16,20},{20,16},{24,28},{28,24},{1,5},{5... | collective-permute-start | bytes 1327112 | tf_op jit(solution)/shard_map/ppermute | solution.py:690
  50.3 5.9 %collective-permute-done.10 = bf16[1,96,2304]{2,1,0:T(8,128)(2,1)S(1)} collective-permute-done((bf16[1,96,2304]{2,1,0:T(8,128)(2,1)S(1)}, bf16[1,96,2304]{2,1,0:T(8,128)(2,1)S(1)}, u32[]{:S(2)}, u32[]{:S(2)}) %collective-permute-start.10) | collective-permute-done | bytes 442400 | tf_op jit(solution)/shard_map/ppermute | solution.py:690
  56.5 1.1 collective-permute-start.11
  57.9 2.1 collective-permute-start.14
  64.2 19.1 %attention_forward.1 = (bf16[1152,2304]{1,0:T(8,128)(2,1)}, bf16[1152,768]{1,0:T(8,128)(2,1)}, bf16[8,6,256,128]{3,2,1,0:T(8,128)(2,1)}, bf16[768,2304]{1,0:T(8,...) custom-call(s32[88]{0:T(128)} %concatenate.62.table, ...), custom_call_target="tpu_custom_call" | custom-call | flops 4831 | bytes 23 | tf_op jit(solution)/shard_map/attention_forward/pallas_call | solution.py:893
  86.4 0.9 copy-done.6
  87.4 23.0 %ffn_forward.1 = (bf16[4,1024,768]{2,1,0:T(8,128)(2,1)}, bf16[4,1024,768]{2,1,0:T(8,128)(2,1)}, f32[1024,768]{1,0:T(8,128)}, f32[1024,128]{1,0:T(8,128)}, bf16[8,768]{1,0:T(8,128)(2,1)}) custom-call(s32[88]{0:T(128)} %concatenate.62.table, f32[1024,768]{1,0:T(8,128)} %get-tuple-element.145.z1_in, f32[1,768]{1,0:T(1,128)} %reshape.678.gain1, ...), custom_call_target="tpu_custom_call" | custom-call | flops 9663 | bytes 31 | tf_op jit(solution)/shard_map/ffn_forward/pallas_call | solution.py:963
  110.4 2.3 collective-permute-start.21
  112.6 1.0 collective-permute-start.22
  113.9 2.4 collective-permute-done.22
  117.8 1.2 collective-permute-start.24
  119.1 1.5 collective-permute-start.26
  120.6 2.6 collective-permute-start.27
  123.2 1.9 collective-permute-start.28
  125.8 1.4 collective-permute-start.30
  130.2 41.1 %ffn_backward.1 = (bf16[4,4,96,768]{3,2,1,0:T(8,128)(2,1)}, bf16[2,4,96,768]{3,2,1,0:T(8,128)(2,1)}, bf16[2,4,96,768]{3,2,1,0:T(8,128)(2,1)}, bf16[4,4,96,768]{3...) custom-call(s32[88]{0:T(128)} %concatenate.62.table, ...), custom_call_target="tpu_custom_call" | custom-call | flops 19327 | bytes 47 | tf_op jit(solution)/shard_map/ffn_backward/pallas_call | solution.py:1002
  173.3 1.1 collective-permute-done.32
  174.4 1.7 fusion
  176.4 1.3 fusion.1
  179.9 3.5 %collective-permute-start.37 = (f32[6,768]{1,0:T(8,128)S(1)}, f32[6,768]{1,0:T(8,128)S(1)}, u32[]{:S(2)}, u32[]{:S(2)}) collective-permute-start(f32[6,768]{1,0:T(8,128)S(1)} %pad_maximum_fusion.12), channel_id=1, source_target_pairs={{0,1},{1,0},{2,3},{3,2},{4,5},{5,4},{6,7},{7,6},{8,9},{9,8},{10,11... | collective-permute-start | bytes 55304 | tf_op jit(solution)/shard_map/ppermute | solution.py:690
  183.4 1.3 slice_bitcast_fusion.3
  184.8 21.4 %attention_backward.1 = (bf16[1152,2304]{1,0:T(8,128)(2,1)}, bf16[8,32,768]{2,1,0:T(8,128)(2,1)}, bf16[8,32,768]{2,1,0:T(8,128)(2,1)}, bf16[8,32,768]{2,1,0:T(8,128)(2,1)}, bf16[8,32,768]{2,1,0:T(8,128)(2,1)}) custom-call(s32[88]{0:T(128)} %concatenate.62.table, bf16[1024,768]{1,0:T(8,128)(2,1)} %get-tuple-element.171.attn_low, ...), custom_call_target="tpu_custom_call" | custom-call | flops 7247 | bytes 23 | tf_op jit(solution)/shard_map/attention_backward/pallas_call | solution.py:1062
  206.3 2.3 fusion.17
  208.5 2.3 fusion.13
  212.5 3.5 %collective-permute-start.41 = (bf16[8,32,768]{2,1,0:T(8,128)(2,1)}, bf16[8,32,768]{2,1,0:T(8,128)(2,1)S(1)}, u32[]{:S(2)}, u32[]{:S(2)}) collective-permute-start(bf16[8,32,768]{2,1,0:T(8,128)(2,1)} %get-tuple-element.200), channel_id=1, source_target_pairs={{0,1},{1,0},{2,3},{3,2},{4,5},{5,4},{6,7},{7,6},{8,9},{9,8},{10,11... | collective-permute-start | bytes 1179656 | tf_op jit(solution)/shard_map/ppermute | solution.py:690
  216.0 9.8 %attention_weights.1 = (bf16[4,4,96,768]{3,2,1,0:T(8,128)(2,1)}, bf16[4,4,96,768]{3,2,1,0:T(8,128)(2,1)}) custom-call(s32[88]{0:T(128)} %concatenate.62.table, bf16[8,96,1024]{2,1,0:T(8,128)(2,1)} %get-tuple-element.192.refs_0_, bf16[8,96,1024]{2,1,0:T(8,128)(2,1)} %get-tuple-element.193.refs_1_, bf16[1152,768]{1,0:T(8,128)(2,1)} %get-tuple-element.194.refs_2_, ...), custom_call_target="tpu_custom_call" | custom-call | flops 4831 | bytes 23 | tf_op jit(solution)/shard_map/attention_weights/pallas_call | solution.py:1099
  225.9 2.4 collective-permute-start.42
  228.3 1.5 fusion.11
  229.8 1.5 fusion.8
  231.5 1.2 collective-permute-done.42
  233.6 2.7 collective-permute-start.46
  236.3 1.0 collective-permute-start.43
  237.6 1.5 collective-permute-start.45
  239.0 18.4 %collective-permute-done.46 = bf16[2,96,1536]{2,1,0:T(8,128)(2,1)S(1)} collective-permute-done((bf16[2,96,1536]{2,1,0:T(8,128)(2,1)S(1)}, bf16[2,96,1536]{2,1,0:T(8,128)(2,1)S(1)}, u32[]{:S(2)}, u32[]{:S(2)}) %collective-permute-start.46) | collective-permute-done | bytes 589856 | tf_op jit(solution)/shard_map/ppermute | solution.py:690
  257.6 2.2 collective-permute-start.47
  259.8 4.2 %collective-permute-done.45 = bf16[4,96,768]{2,1,0:T(8,128)(2,1)S(1)} collective-permute-done((bf16[4,96,768]{2,1,0:T(8,128)(2,1)S(1)}, bf16[4,96,768]{2,1,0:T(8,128)(2,1)S(1)}, u32[]{:S(2)}, u32[]{:S(2)}) %collective-permute-start.45) | collective-permute-done | bytes 589856 | tf_op jit(solution)/shard_map/ppermute | solution.py:690
  264.1 8.5 %collective-permute-done.47 = bf16[1,96,1536]{2,1,0:T(8,128)(2,1)S(1)} collective-permute-done((bf16[1,96,1536]{2,1,0:T(8,128)(2,1)S(1)}, bf16[1,96,1536]{2,1,0:T(8,128)(2,1)S(1)}, u32[]{:S(2)}, u32[]{:S(2)}) %collective-permute-start.47) | collective-permute-done | bytes 294944 | tf_op jit(solution)/shard_map/ppermute | solution.py:690
  273.2 2.4 collective-permute-start.49
  276.8 1.5 collective-permute-start.54
  278.2 4.3 %collective-permute-done.49 = bf16[2,96,768]{2,1,0:T(8,128)(2,1)S(1)} collective-permute-done((bf16[2,96,768]{2,1,0:T(8,128)(2,1)S(1)}, bf16[2,96,768]{2,1,0:T(8,128)(2,1)S(1)}, u32[]{:S(2)}, u32[]{:S(2)}) %collective-permute-start.49) | collective-permute-done | bytes 294944 | tf_op jit(solution)/shard_map/ppermute | solution.py:690
  282.6 1.9 collective-permute-start.50
  285.5 4.7 %collective-permute-done.51 = f32[5,768]{1,0:T(8,128)S(1)} collective-permute-done((f32[5,768]{1,0:T(8,128)S(1)}, f32[5,768]{1,0:T(8,128)S(1)}, u32[]{:S(2)}, u32[]{:S(2)}) %collective-permute-start.51) | collective-permute-done | bytes 15392 | tf_op jit(solution)/shard_map/ppermute | solution.py:690
  290.2 1.0 collective-permute-done.50
  291.5 1.1 collective-permute-start.55
  292.6 1.0 collective-permute-start.56
  295.1 1.2 collective-permute-start.60
  297.3 4.9 %place_grads.1 = (f32[768,768]{1,0:T(8,128)}, f32[768,768]{1,0:T(8,128)}) custom-call(s32[88]{0:T(128)} %concatenate.62.table, bf16[4,96,1536]{2,1,0:T(8,128)(2,1)} %copy-done.3, bf16[4,96,1536]{2,1,0:T(8,128)(2,1)} %copy-done.12), custom_call_target="tpu_custom_call" | custom-call | bytes 9 | tf_op jit(solution)/shard_map/place_grads/pallas_call | solution.py:1119
  302.2 8.7 %collective-permute-done.56.refs_3_ = bf16[8,32,768]{2,1,0:T(8,128)(2,1)S(1)} collective-permute-done((bf16[8,32,768]{2,1,0:T(8,128)(2,1)S(1)}, bf16[8,32,768]{2,1,0:T(8,128)(2,1)S(1)}, u32[]{:S(2)}, u32[]{:S(2)}) %collective-permute-start.56) | collective-permute-done | bytes 393248 | tf_op jit(solution)/shard_map/ppermute | solution.py:690
  311.0 1.7 collective-permute-start.61
  313.8 3.6 %send_home.1 = bf16[32,32,768]{2,1,0:T(8,128)(2,1)} custom-call(s32[512,1]{1,0:T(8,128)} %reshape_tile.4.source, bf16[8,32,768]{2,1,0:T(8,128)(2,1)} %get-tuple-element.191.refs_0_, bf16[8,32,768]{2,1,0:T(8,128)(2,1)} %copy-done.23, bf16[8,32,768]{2,1,0:T(8,128)(2,1)} %copy-done.24, bf16[8,32,768]{2,1,0:T(8,128)(2,1)} %copy-done.25), custom_call_target="tpu_custom_call" | custom-call | bytes 3 | tf_op jit(solution)/shard_map/send_home/pallas_call | solution.py:1183
  318.9 4.1 %place_attention_grads.1 = (f32[576,768]{1,0:T(8,128)}, f32[192,768]{1,0:T(8,128)}) custom-call(s32[88]{0:T(128)} %concatenate.62.table, bf16[4,96,768]{2,1,0:T(8,128)(2,1)} %copy-done.9, bf16[4,96,768]{2,1,0:T(8,128)(2,1)} %copy-done.13), custom_call_target="tpu_custom_call" | custom-call | bytes 4 | tf_op jit(solution)/shard_map/place_attention_grads/pallas_call | solution.py:1119
  (252 shorter events, 36.2 us)
Async XLA Ops:
  3.2 9.4 %collective-permute-start = (bf16[96,768]{1,0:T(8,128)(2,1)S(1)}, bf16[96,768]{1,0:T(8,128)(2,1)S(1)}, u32[]{:S(2)}, u32[]{:S(2)}) collective-permute-start(bf16[96,768]{1,0:T(8,128)(2,1)S(1)} %pad_maximum_fusion.10), channel_id=1, source_target_pairs={{0,2},{1,3},{2,0},{3,1},{4,6},{5,7},{6,4},{7,5},{8,10},{9,11},{10,... | collective-permute-start | bytes 442376 | tf_op jit(solution)/shard_map/ppermute | solution.py:690
  7.3 8.3 %collective-permute-start.5 = (bf16[96,1536]{1,0:T(8,128)(2,1)S(1)}, bf16[96,1536]{1,0:T(8,128)(2,1)S(1)}, u32[]{:S(2)}, u32[]{:S(2)}) collective-permute-start(bf16[96,1536]{1,0:T(8,128)(2,1)S(1)} %pad_maximum_fusion.9), channel_id=1, source_target_pairs={{0,1},{1,0},{2,3},{3,2},{4,5},{5,4},{6,7},{7,6},{8,9},{9,8},{10,11... | collective-permute-start | bytes 884744 | tf_op jit(solution)/shard_map/ppermute | solution.py:690
  7.5 10.6 %collective-permute-start.7 = (f32[1,768]{1,0:T(1,128)S(1)}, f32[1,768]{1,0:T(1,128)S(1)}, u32[]{:S(2)}, u32[]{:S(2)}) collective-permute-start(f32[1,768]{1,0:T(1,128)S(1)} %reshape.677), channel_id=1, source_target_pairs={{0,1},{1,0},{2,3},{3,2},{4,5},{5,4},{6,7},{7,6},{8,9},{9,8},{10,11... | collective-permute-start | bytes 9224 | tf_op jit(solution)/shard_map/ppermute | solution.py:690
  12.6 12.1 %collective-permute-start.1 = (bf16[96,1536]{1,0:T(8,128)(2,1)S(1)}, bf16[96,1536]{1,0:T(8,128)(2,1)S(1)}, u32[]{:S(2)}, u32[]{:S(2)}) collective-permute-start(bf16[96,1536]{1,0:T(8,128)(2,1)S(1)} %pad_maximum_fusion.8), channel_id=1, source_target_pairs={{0,1},{1,0},{2,3},{3,2},{4,5},{5,4},{6,7},{7,6},{8,9},{9,8},{10,11... | collective-permute-start | bytes 884744 | tf_op jit(solution)/shard_map/ppermute | solution.py:690
  15.6 25.7 %collective-permute-start.6 = (bf16[96,3072]{1,0:T(8,128)(2,1)S(1)}, bf16[96,3072]{1,0:T(8,128)(2,1)S(1)}, u32[]{:S(2)}, u32[]{:S(2)}) collective-permute-start(bf16[96,3072]{1,0:T(8,128)(2,1)S(1)} %pad_maximum_fusion.4), channel_id=1, source_target_pairs={{0,2},{1,3},{2,0},{3,1},{4,6},{5,7},{6,4},{7,5},{8,10},{9,11},{10,... | collective-permute-start | bytes 1769480 | tf_op jit(solution)/shard_map/ppermute | solution.py:690
  18.2 23.2 %collective-permute-start.8 = (f32[1,1536]{1,0:T(1,128)S(1)}, f32[1,1536]{1,0:T(1,128)S(1)}, u32[]{:S(2)}, u32[]{:S(2)}) collective-permute-start(f32[1,1536]{1,0:T(1,128)S(1)} %pad_maximum_fusion.16), channel_id=1, source_target_pairs={{0,2},{1,3},{2,0},{3,1},{4,6},{5,7},{6,4},{7,5},{8,10},{9,11},{10,... | collective-permute-start | bytes 18440 | tf_op jit(solution)/shard_map/ppermute | solution.py:690
  24.8 18.7 %collective-permute-start.2 = (bf16[96,2304]{1,0:T(8,128)(2,1)S(1)}, bf16[96,2304]{1,0:T(8,128)(2,1)S(1)}, u32[]{:S(2)}, u32[]{:S(2)}) collective-permute-start(bf16[96,2304]{1,0:T(8,128)(2,1)S(1)} %pad_maximum_fusion.7.refs_0_), channel_id=1, source_target_pairs={{0,8},{4,12},{8,0},{12,4},{16,24},{20,28},{24,16},{28,20},{1,9},{5... | collective-permute-start | bytes 1327112 | tf_op jit(solution)/shard_map/ppermute | solution.py:690
  26.0 17.4 %collective-permute-start.3 = (bf16[96,2304]{1,0:T(8,128)(2,1)S(1)}, bf16[96,2304]{1,0:T(8,128)(2,1)S(1)}, u32[]{:S(2)}, u32[]{:S(2)}) collective-permute-start(bf16[96,2304]{1,0:T(8,128)(2,1)S(1)} %pad_maximum_fusion.7.refs_0_), channel_id=1, source_target_pairs={{0,16},{4,20},{8,24},{12,28},{16,0},{20,4},{24,8},{28,12},{1,17},{... | collective-permute-start | bytes 1327112 | tf_op jit(solution)/shard_map/ppermute | solution.py:690
  27.1 18.8 %collective-permute-start.4 = (bf16[96,2304]{1,0:T(8,128)(2,1)S(1)}, bf16[96,2304]{1,0:T(8,128)(2,1)}, u32[]{:S(2)}, u32[]{:S(2)}) collective-permute-start(bf16[96,2304]{1,0:T(8,128)(2,1)S(1)} %pad_maximum_fusion.7.refs_0_), channel_id=1, source_target_pairs={{0,24},{4,28},{8,16},{12,20},{16,8},{20,12},{24,0},{28,4},{1,25},{... | collective-permute-start | bytes 1327112 | tf_op jit(solution)/shard_map/ppermute | solution.py:690
  41.4 14.9 %collective-permute-start.10 = (bf16[1,96,2304]{2,1,0:T(8,128)(2,1)S(1)}, bf16[1,96,2304]{2,1,0:T(8,128)(2,1)S(1)}, u32[]{:S(2)}, u32[]{:S(2)}) collective-permute-start(bf16[1,96,2304]{2,1,0:T(8,128)(2,1)S(1)} %get-tuple-element.261), channel_id=1, source_target_pairs={{0,16},{4,20},{8,24},{12,28},{16,0},{20,4},{24,8},{28,12},{1,17},{... | collective-permute-start | bytes 1327112 | tf_op jit(solution)/shard_map/ppermute | solution.py:690
  42.7 13.7 %collective-permute-start.9 = (bf16[1,96,2304]{2,1,0:T(8,128)(2,1)S(1)}, bf16[1,96,2304]{2,1,0:T(8,128)(2,1)S(1)}, u32[]{:S(2)}, u32[]{:S(2)}) collective-permute-start(bf16[1,96,2304]{2,1,0:T(8,128)(2,1)S(1)} %get-tuple-element.262), channel_id=1, source_target_pairs={{0,8},{4,12},{8,0},{12,4},{16,24},{20,28},{24,16},{28,20},{1,9},{5... | collective-permute-start | bytes 1327112 | tf_op jit(solution)/shard_map/ppermute | solution.py:690
  45.9 14.1 %collective-permute-start.13 = (bf16[96,2304]{1,0:T(8,128)(2,1)S(1)}, bf16[96,2304]{1,0:T(8,128)(2,1)S(1)}, u32[]{:S(2)}, u32[]{:S(2)}) collective-permute-start(bf16[96,2304]{1,0:T(8,128)(2,1)S(1)} %pad_maximum_fusion.7.refs_0_), channel_id=1, source_target_pairs={{0,4},{4,0},{8,12},{12,8},{16,20},{20,16},{24,28},{28,24},{1,5},{5... | collective-permute-start | bytes 1327112 | tf_op jit(solution)/shard_map/ppermute | solution.py:690
  56.5 26.9 %collective-permute-start.11 = (bf16[2,96,2304]{2,1,0:T(8,128)(2,1)S(1)}, bf16[2,96,2304]{2,1,0:T(8,128)(2,1)S(1)}, u32[]{:S(2)}, u32[]{:S(2)}) collective-permute-start(bf16[2,96,2304]{2,1,0:T(8,128)(2,1)S(1)} %pad_maximum_fusion.1.refs_0_), channel_id=1, source_target_pairs={{0,16},{4,20},{8,24},{12,28},{16,0},{20,4},{24,8},{28,12},{1,17},{... | collective-permute-start | bytes 2654216 | tf_op jit(solution)/shard_map/ppermute | solution.py:690
  57.6 25.8 %collective-permute-start.12 = (bf16[2,96,2304]{2,1,0:T(8,128)(2,1)S(1)}, bf16[2,96,2304]{2,1,0:T(8,128)(2,1)S(1)}, u32[]{:S(2)}, u32[]{:S(2)}) collective-permute-start(bf16[2,96,2304]{2,1,0:T(8,128)(2,1)S(1)} %pad_maximum_fusion.2.refs_2_), channel_id=1, source_target_pairs={{0,8},{4,12},{8,0},{12,4},{16,24},{20,28},{24,16},{28,20},{1,9},{5... | collective-permute-start | bytes 2654216 | tf_op jit(solution)/shard_map/ppermute | solution.py:690
  57.9 3.5 %collective-permute-start.14 = (bf16[96,2304]{1,0:T(8,128)(2,1)S(1)}, bf16[96,2304]{1,0:T(8,128)(2,1)S(1)}, u32[]{:S(2)}, u32[]{:S(2)}) collective-permute-start(bf16[96,2304]{1,0:T(8,128)(2,1)S(1)} %copy-done.15), channel_id=1, source_target_pairs={{0,4},{4,0},{8,12},{12,8},{16,20},{20,16},{24,28},{28,24},{1,5},{5... | collective-permute-start | bytes 1327112 | tf_op jit(solution)/shard_map/ppermute | solution.py:690
  59.9 2.7 collective-permute-start.15
  60.0 3.0 collective-permute-start.16
  61.4 25.0 %collective-permute-start.17 = (bf16[2,96,2304]{2,1,0:T(8,128)(2,1)S(1)}, bf16[2,96,2304]{2,1,0:T(8,128)(2,1)}, u32[]{:S(2)}, u32[]{:S(2)}) collective-permute-start(bf16[2,96,2304]{2,1,0:T(8,128)(2,1)S(1)} %pad_maximum_fusion.1.refs_0_), channel_id=1, source_target_pairs={{0,4},{4,0},{8,12},{12,8},{16,20},{20,16},{24,28},{28,24},{1,5},{5... | collective-permute-start | bytes 2654216 | tf_op jit(solution)/shard_map/ppermute | solution.py:690
  62.6 23.8 %collective-permute-start.19 = (bf16[2,96,2304]{2,1,0:T(8,128)(2,1)S(1)}, bf16[2,96,2304]{2,1,0:T(8,128)(2,1)}, u32[]{:S(2)}, u32[]{:S(2)}) collective-permute-start(bf16[2,96,2304]{2,1,0:T(8,128)(2,1)S(1)} %pad_maximum_fusion.2.refs_2_), channel_id=1, source_target_pairs={{0,4},{4,0},{8,12},{12,8},{16,20},{20,16},{24,28},{28,24},{1,5},{5... | collective-permute-start | bytes 2654216 | tf_op jit(solution)/shard_map/ppermute | solution.py:690
  83.4 3.0 collective-permute-start.18
  83.9 3.5 %collective-permute-start.20 = (bf16[2,96,2304]{2,1,0:T(8,128)(2,1)S(1)}, bf16[2,96,2304]{2,1,0:T(8,128)(2,1)}, u32[]{:S(2)}, u32[]{:S(2)}) collective-permute-start(bf16[2,96,2304]{2,1,0:T(8,128)(2,1)S(1)} %collective-permute-done.12.refs_3_), channel_id=1, source_target_pairs={{0,4},{4,0},{8,12},{12,8},{16,20},{20,16},{24,28},{28,24},{1,5},{5... | collective-permute-start | bytes 2654216 | tf_op jit(solution)/shard_map/ppermute | solution.py:690
  86.4 31.4 %copy-start.26 = (bf16[32,768]{1,0:T(8,128)(2,1)S(1)}, bf16[32,768]{1,0:T(8,128)(2,1)}, u32[]{:S(2)}) copy-start(bf16[32,768]{1,0:T(8,128)(2,1)} %param.35) | copy-start | bytes 147460
  110.4 3.6 %collective-permute-start.21 = (bf16[8,768]{1,0:T(8,128)(2,1)}, bf16[8,768]{1,0:T(8,128)(2,1)S(1)}, u32[]{:S(2)}, u32[]{:S(2)}) collective-permute-start(bf16[8,768]{1,0:T(8,128)(2,1)} %get-tuple-element.149), channel_id=1, source_target_pairs={{0,1},{1,0},{2,3},{3,2},{4,5},{5,4},{6,7},{7,6},{8,9},{9,8},{10,11... | collective-permute-start | bytes 36872 | tf_op jit(solution)/shard_map/ppermute | solution.py:690
  112.6 3.7 %collective-permute-start.22 = (bf16[8,768]{1,0:T(8,128)(2,1)}, bf16[8,768]{1,0:T(8,128)(2,1)S(1)}, u32[]{:S(2)}, u32[]{:S(2)}) collective-permute-start(bf16[8,768]{1,0:T(8,128)(2,1)} %get-tuple-element.149), channel_id=1, source_target_pairs={{0,2},{1,3},{2,0},{3,1},{4,6},{5,7},{6,4},{7,5},{8,10},{9,11},{10,... | collective-permute-start | bytes 36872 | tf_op jit(solution)/shard_map/ppermute | solution.py:690
  113.6 2.8 collective-permute-start.23
  117.8 5.4 %collective-permute-start.24 = (bf16[64,768]{1,0:T(8,128)(2,1)S(1)}, bf16[64,768]{1,0:T(8,128)(2,1)S(1)}, u32[]{:S(2)}, u32[]{:S(2)}) collective-permute-start(bf16[64,768]{1,0:T(8,128)(2,1)S(1)} %constant_dynamic-update-slice_fusion), channel_id=1, source_target_pairs={{0,8},{4,12},{8,0},{12,4},{16,24},{20,28},{24,16},{28,20},{1,9},{5... | collective-permute-start | bytes 294920 | tf_op jit(solution)/shard_map/ppermute | solution.py:690
  119.0 6.2 %collective-permute-start.25 = (bf16[64,768]{1,0:T(8,128)(2,1)S(1)}, bf16[64,768]{1,0:T(8,128)(2,1)S(1)}, u32[]{:S(2)}, u32[]{:S(2)}) collective-permute-start(bf16[64,768]{1,0:T(8,128)(2,1)S(1)} %constant_dynamic-update-slice_fusion), channel_id=1, source_target_pairs={{0,16},{4,20},{8,24},{12,28},{16,0},{20,4},{24,8},{28,12},{1,17},{... | collective-permute-start | bytes 294920 | tf_op jit(solution)/shard_map/ppermute | solution.py:690
  119.1 6.7 %collective-permute-start.26 = (bf16[64,768]{1,0:T(8,128)(2,1)S(1)}, bf16[64,768]{1,0:T(8,128)(2,1)S(1)}, u32[]{:S(2)}, u32[]{:S(2)}) collective-permute-start(bf16[64,768]{1,0:T(8,128)(2,1)S(1)} %constant_dynamic-update-slice_fusion), channel_id=1, source_target_pairs={{0,24},{4,28},{8,16},{12,20},{16,8},{20,12},{24,0},{28,4},{1,25},{... | collective-permute-start | bytes 294920 | tf_op jit(solution)/shard_map/ppermute | solution.py:690
  120.6 6.7 %collective-permute-start.27 = (bf16[64,768]{1,0:T(8,128)(2,1)S(1)}, bf16[64,768]{1,0:T(8,128)(2,1)S(1)}, u32[]{:S(2)}, u32[]{:S(2)}) collective-permute-start(bf16[64,768]{1,0:T(8,128)(2,1)S(1)} %constant_dynamic-update-slice_fusion), channel_id=1, source_target_pairs={{0,4},{4,0},{8,12},{12,8},{16,20},{20,16},{24,28},{28,24},{1,5},{5... | collective-permute-start | bytes 294920 | tf_op jit(solution)/shard_map/ppermute | solution.py:690
  123.2 4.1 %collective-permute-start.28 = (bf16[64,768]{1,0:T(8,128)(2,1)S(1)}, bf16[64,768]{1,0:T(8,128)(2,1)S(1)}, u32[]{:S(2)}, u32[]{:S(2)}) collective-permute-start(bf16[64,768]{1,0:T(8,128)(2,1)S(1)} %collective-permute-done.24), channel_id=1, source_target_pairs={{0,4},{4,0},{8,12},{12,8},{16,20},{20,16},{24,28},{28,24},{1,5},{5... | collective-permute-start | bytes 294920 | tf_op jit(solution)/shard_map/ppermute | solution.py:690
  125.2 2.1 collective-permute-start.29
  125.8 2.4 collective-permute-start.30
  171.3 3.1 collective-permute-start.32
  171.7 4.4 %collective-permute-start.31 = (bf16[2,4,96,768]{3,2,1,0:T(8,128)(2,1)}, bf16[2,4,96,768]{3,2,1,0:T(8,128)(2,1)S(1)}, u32[]{:S(2)}, u32[]{:S(2)}) collective-permute-start(bf16[2,4,96,768]{3,2,1,0:T(8,128)(2,1)} %get-tuple-element.156), channel_id=1, source_target_pairs={{0,4},{4,0},{8,12},{12,8},{16,20},{20,16},{24,28},{28,24},{1,5},{5... | collective-permute-start | bytes 3538952 | tf_op jit(solution)/shard_map/ppermute | solution.py:690
  177.8 28.4 %collective-permute-start.35 = (bf16[2,4,96,768]{3,2,1,0:T(8,128)(2,1)}, bf16[2,4,96,768]{3,2,1,0:T(8,128)(2,1)}, u32[]{:S(2)}, u32[]{:S(2)}) collective-permute-start(bf16[2,4,96,768]{3,2,1,0:T(8,128)(2,1)} %get-tuple-element.168), channel_id=1, source_target_pairs={{0,4},{4,0},{8,12},{12,8},{16,20},{20,16},{24,28},{28,24},{1,5},{5... | collective-permute-start | bytes 3538952 | tf_op jit(solution)/shard_map/ppermute | solution.py:690
  178.1 28.1 %collective-permute-start.36 = (bf16[2,4,96,768]{3,2,1,0:T(8,128)(2,1)}, bf16[2,4,96,768]{3,2,1,0:T(8,128)(2,1)}, u32[]{:S(2)}, u32[]{:S(2)}) collective-permute-start(bf16[2,4,96,768]{3,2,1,0:T(8,128)(2,1)} %get-tuple-element.169), channel_id=1, source_target_pairs={{0,4},{4,0},{8,12},{12,8},{16,20},{20,16},{24,28},{28,24},{1,5},{5... | collective-permute-start | bytes 3538952 | tf_op jit(solution)/shard_map/ppermute | solution.py:690
  178.3 27.9 %collective-permute-start.33 = (bf16[2,4,96,768]{3,2,1,0:T(8,128)(2,1)}, bf16[2,4,96,768]{3,2,1,0:T(8,128)(2,1)}, u32[]{:S(2)}, u32[]{:S(2)}) collective-permute-start(bf16[2,4,96,768]{3,2,1,0:T(8,128)(2,1)} %fusion.1), channel_id=1, source_target_pairs={{0,8},{4,12},{8,0},{12,4},{16,24},{20,28},{24,16},{28,20},{1,9},{5... | collective-permute-start | bytes 3538952 | tf_op jit(solution)/shard_map/ppermute | solution.py:690
  179.2 27.0 %collective-permute-start.34 = (bf16[2,4,96,768]{3,2,1,0:T(8,128)(2,1)S(1)}, bf16[2,4,96,768]{3,2,1,0:T(8,128)(2,1)}, u32[]{:S(2)}, u32[]{:S(2)}) collective-permute-start(bf16[2,4,96,768]{3,2,1,0:T(8,128)(2,1)S(1)} %fusion), channel_id=1, source_target_pairs={{0,16},{4,20},{8,24},{12,28},{16,0},{20,4},{24,8},{28,12},{1,17},{... | collective-permute-start | bytes 3538952 | tf_op jit(solution)/shard_map/ppermute | solution.py:690
  179.9 26.3 %collective-permute-start.37 = (f32[6,768]{1,0:T(8,128)S(1)}, f32[6,768]{1,0:T(8,128)S(1)}, u32[]{:S(2)}, u32[]{:S(2)}) collective-permute-start(f32[6,768]{1,0:T(8,128)S(1)} %pad_maximum_fusion.12), channel_id=1, source_target_pairs={{0,1},{1,0},{2,3},{3,2},{4,5},{5,4},{6,7},{7,6},{8,9},{9,8},{10,11... | collective-permute-start | bytes 55304 | tf_op jit(solution)/shard_map/ppermute | solution.py:690
  210.8 15.1 %collective-permute-start.39 = (bf16[1,4,96,768]{3,2,1,0:T(8,128)(2,1)}, bf16[1,4,96,768]{3,2,1,0:T(8,128)(2,1)S(1)}, u32[]{:S(2)}, u32[]{:S(2)}) collective-permute-start(bf16[1,4,96,768]{3,2,1,0:T(8,128)(2,1)} %fusion.13), channel_id=1, source_target_pairs={{0,16},{4,20},{8,24},{12,28},{16,0},{20,4},{24,8},{28,12},{1,17},{... | collective-permute-start | bytes 1769480 | tf_op jit(solution)/shard_map/ppermute | solution.py:690
  211.7 14.1 %collective-permute-start.40 = (bf16[1,4,96,768]{3,2,1,0:T(8,128)(2,1)}, bf16[1,4,96,768]{3,2,1,0:T(8,128)(2,1)S(1)}, u32[]{:S(2)}, u32[]{:S(2)}) collective-permute-start(bf16[1,4,96,768]{3,2,1,0:T(8,128)(2,1)} %fusion.17), channel_id=1, source_target_pairs={{0,8},{4,12},{8,0},{12,4},{16,24},{20,28},{24,16},{28,20},{1,9},{5... | collective-permute-start | bytes 1769480 | tf_op jit(solution)/shard_map/ppermute | solution.py:690
  212.5 13.4 %collective-permute-start.41 = (bf16[8,32,768]{2,1,0:T(8,128)(2,1)}, bf16[8,32,768]{2,1,0:T(8,128)(2,1)S(1)}, u32[]{:S(2)}, u32[]{:S(2)}) collective-permute-start(bf16[8,32,768]{2,1,0:T(8,128)(2,1)} %get-tuple-element.200), channel_id=1, source_target_pairs={{0,1},{1,0},{2,3},{3,2},{4,5},{5,4},{6,7},{7,6},{8,9},{9,8},{10,11... | collective-permute-start | bytes 1179656 | tf_op jit(solution)/shard_map/ppermute | solution.py:690
  216.0 9.9 %collective-permute-start.38 = (f32[5,768]{1,0:T(8,128)S(1)}, f32[5,768]{1,0:T(8,128)S(1)}, u32[]{:S(2)}, u32[]{:S(2)}) collective-permute-start(f32[5,768]{1,0:T(8,128)S(1)} %pad_maximum_fusion.13), channel_id=1, source_target_pairs={{0,2},{1,3},{2,0},{3,1},{4,6},{5,7},{6,4},{7,5},{8,10},{9,11},{10,... | collective-permute-start | bytes 46088 | tf_op jit(solution)/shard_map/ppermute | solution.py:690
  225.9 6.8 %collective-permute-start.42 = (bf16[4,4,96,768]{3,2,1,0:T(8,128)(2,1)}, bf16[4,4,96,768]{3,2,1,0:T(8,128)(2,1)S(1)}, u32[]{:S(2)}, u32[]{:S(2)}) collective-permute-start(bf16[4,4,96,768]{3,2,1,0:T(8,128)(2,1)} %get-tuple-element.202), channel_id=1, source_target_pairs={{0,4},{4,0},{8,12},{12,8},{16,20},{20,16},{24,28},{28,24},{1,5},{5... | collective-permute-start | bytes 7077896 | tf_op jit(solution)/shard_map/ppermute | solution.py:690
  233.6 23.9 %collective-permute-start.46 = (bf16[2,96,1536]{2,1,0:T(8,128)(2,1)S(1)}, bf16[2,96,1536]{2,1,0:T(8,128)(2,1)S(1)}, u32[]{:S(2)}, u32[]{:S(2)}) collective-permute-start(bf16[2,96,1536]{2,1,0:T(8,128)(2,1)S(1)} %get-tuple-element.210), channel_id=1, source_target_pairs={{0,1},{1,0},{2,3},{3,2},{4,5},{5,4},{6,7},{7,6},{8,9},{9,8},{10,11... | collective-permute-start | bytes 1769480 | tf_op jit(solution)/shard_map/ppermute | solution.py:690
  236.3 23.5 %collective-permute-start.43 = (bf16[4,96,768]{2,1,0:T(8,128)(2,1)S(1)}, bf16[4,96,768]{2,1,0:T(8,128)(2,1)S(1)}, u32[]{:S(2)}, u32[]{:S(2)}) collective-permute-start(bf16[4,96,768]{2,1,0:T(8,128)(2,1)S(1)} %get-tuple-element.207), channel_id=1, source_target_pairs={{0,8},{4,12},{8,0},{12,4},{16,24},{20,28},{24,16},{28,20},{1,9},{5... | collective-permute-start | bytes 1769480 | tf_op jit(solution)/shard_map/ppermute | solution.py:690
  237.3 22.5 %collective-permute-start.44 = (bf16[4,96,768]{2,1,0:T(8,128)(2,1)S(1)}, bf16[4,96,768]{2,1,0:T(8,128)(2,1)S(1)}, u32[]{:S(2)}, u32[]{:S(2)}) collective-permute-start(bf16[4,96,768]{2,1,0:T(8,128)(2,1)S(1)} %get-tuple-element.208), channel_id=1, source_target_pairs={{0,16},{4,20},{8,24},{12,28},{16,0},{20,4},{24,8},{28,12},{1,17},{... | collective-permute-start | bytes 1769480 | tf_op jit(solution)/shard_map/ppermute | solution.py:690
  237.6 26.5 %collective-permute-start.45 = (bf16[4,96,768]{2,1,0:T(8,128)(2,1)S(1)}, bf16[4,96,768]{2,1,0:T(8,128)(2,1)S(1)}, u32[]{:S(2)}, u32[]{:S(2)}) collective-permute-start(bf16[4,96,768]{2,1,0:T(8,128)(2,1)S(1)} %get-tuple-element.209), channel_id=1, source_target_pairs={{0,24},{4,28},{8,16},{12,20},{16,8},{20,12},{24,0},{28,4},{1,25},{... | collective-permute-start | bytes 1769480 | tf_op jit(solution)/shard_map/ppermute | solution.py:690
  239.0 20.8 %collective-permute-start.48 = (bf16[8,32,768]{2,1,0:T(8,128)(2,1)S(1)}, bf16[8,32,768]{2,1,0:T(8,128)(2,1)S(1)}, u32[]{:S(2)}, u32[]{:S(2)}) collective-permute-start(bf16[8,32,768]{2,1,0:T(8,128)(2,1)S(1)} %copy-done.41), channel_id=1, source_target_pairs={{0,2},{1,3},{2,0},{3,1},{4,6},{5,7},{6,4},{7,5},{8,10},{9,11},{10,... | collective-permute-start | bytes 1179656 | tf_op jit(solution)/shard_map/ppermute | solution.py:690
  257.6 15.0 %collective-permute-start.47 = (bf16[1,96,1536]{2,1,0:T(8,128)(2,1)S(1)}, bf16[1,96,1536]{2,1,0:T(8,128)(2,1)S(1)}, u32[]{:S(2)}, u32[]{:S(2)}) collective-permute-start(bf16[1,96,1536]{2,1,0:T(8,128)(2,1)S(1)} %fusion.23), channel_id=1, source_target_pairs={{0,2},{1,3},{2,0},{3,1},{4,6},{5,7},{6,4},{7,5},{8,10},{9,11},{10,... | collective-permute-start | bytes 884744 | tf_op jit(solution)/shard_map/ppermute | solution.py:690
  273.2 9.4 %collective-permute-start.49 = (bf16[2,96,768]{2,1,0:T(8,128)(2,1)S(1)}, bf16[2,96,768]{2,1,0:T(8,128)(2,1)S(1)}, u32[]{:S(2)}, u32[]{:S(2)}) collective-permute-start(bf16[2,96,768]{2,1,0:T(8,128)(2,1)S(1)} %get-tuple-element.220), channel_id=1, source_target_pairs={{0,1},{1,0},{2,3},{3,2},{4,5},{5,4},{6,7},{7,6},{8,9},{9,8},{10,11... | collective-permute-start | bytes 884744 | tf_op jit(solution)/shard_map/ppermute | solution.py:690
  275.6 14.6 %collective-permute-start.52 = (bf16[96,1536]{1,0:T(8,128)(2,1)S(1)}, bf16[96,1536]{1,0:T(8,128)(2,1)S(1)}, u32[]{:S(2)}, u32[]{:S(2)}) collective-permute-start(bf16[96,1536]{1,0:T(8,128)(2,1)S(1)} %fusion.24), channel_id=1, source_target_pairs={{0,8},{4,12},{8,0},{12,4},{16,24},{20,28},{24,16},{28,20},{1,9},{5... | collective-permute-start | bytes 884744 | tf_op jit(solution)/shard_map/ppermute | solution.py:690
  276.5 13.7 %collective-permute-start.53 = (bf16[96,1536]{1,0:T(8,128)(2,1)S(1)}, bf16[96,1536]{1,0:T(8,128)(2,1)S(1)}, u32[]{:S(2)}, u32[]{:S(2)}) collective-permute-start(bf16[96,1536]{1,0:T(8,128)(2,1)S(1)} %fusion.24), channel_id=1, source_target_pairs={{0,16},{4,20},{8,24},{12,28},{16,0},{20,4},{24,8},{28,12},{1,17},{... | collective-permute-start | bytes 884744 | tf_op jit(solution)/shard_map/ppermute | solution.py:690
  276.8 13.4 %collective-permute-start.54 = (bf16[96,1536]{1,0:T(8,128)(2,1)S(1)}, bf16[96,1536]{1,0:T(8,128)(2,1)S(1)}, u32[]{:S(2)}, u32[]{:S(2)}) collective-permute-start(bf16[96,1536]{1,0:T(8,128)(2,1)S(1)} %fusion.24), channel_id=1, source_target_pairs={{0,24},{4,28},{8,16},{12,20},{16,8},{20,12},{24,0},{28,4},{1,25},{... | collective-permute-start | bytes 884744 | tf_op jit(solution)/shard_map/ppermute | solution.py:690
  282.6 8.6 %collective-permute-start.50 = (bf16[1,96,768]{2,1,0:T(8,128)(2,1)S(1)}, bf16[1,96,768]{2,1,0:T(8,128)(2,1)S(1)}, u32[]{:S(2)}, u32[]{:S(2)}) collective-permute-start(bf16[1,96,768]{2,1,0:T(8,128)(2,1)S(1)} %fusion.26), channel_id=1, source_target_pairs={{0,2},{1,3},{2,0},{3,1},{4,6},{5,7},{6,4},{7,5},{8,10},{9,11},{10,... | collective-permute-start | bytes 442376 | tf_op jit(solution)/shard_map/ppermute | solution.py:690
  284.5 5.7 %collective-permute-start.51 = (f32[5,768]{1,0:T(8,128)S(1)}, f32[5,768]{1,0:T(8,128)S(1)}, u32[]{:S(2)}, u32[]{:S(2)}) collective-permute-start(f32[5,768]{1,0:T(8,128)S(1)} %pad_maximum_fusion.14), channel_id=1, source_target_pairs={{0,8},{4,12},{8,0},{12,4},{16,24},{20,28},{24,16},{28,20},{1,9},{5... | collective-permute-start | bytes 46088 | tf_op jit(solution)/shard_map/ppermute | solution.py:690
  291.5 4.8 %collective-permute-start.55 = (bf16[4,96,1536]{2,1,0:T(8,128)(2,1)S(1)}, bf16[4,96,1536]{2,1,0:T(8,128)(2,1)S(1)}, u32[]{:S(2)}, u32[]{:S(2)}) collective-permute-start(bf16[4,96,1536]{2,1,0:T(8,128)(2,1)S(1)} %pad_maximum_fusion.near), channel_id=1, source_target_pairs={{0,4},{4,0},{8,12},{12,8},{16,20},{20,16},{24,28},{28,24},{1,5},{5... | collective-permute-start | bytes 3538952 | tf_op jit(solution)/shard_map/ppermute | solution.py:690
  292.6 18.3 %collective-permute-start.56 = (bf16[8,32,768]{2,1,0:T(8,128)(2,1)S(1)}, bf16[8,32,768]{2,1,0:T(8,128)(2,1)S(1)}, u32[]{:S(2)}, u32[]{:S(2)}) collective-permute-start(bf16[8,32,768]{2,1,0:T(8,128)(2,1)S(1)} %copy-done.40), channel_id=1, source_target_pairs={{0,3},{1,2},{2,1},{3,0},{4,7},{5,6},{6,5},{7,4},{8,11},{9,10},{10,... | collective-permute-start | bytes 1179656 | tf_op jit(solution)/shard_map/ppermute | solution.py:690
  293.6 17.3 %collective-permute-start.58 = (bf16[96,768]{1,0:T(8,128)(2,1)S(1)}, bf16[96,768]{1,0:T(8,128)(2,1)S(1)}, u32[]{:S(2)}, u32[]{:S(2)}) collective-permute-start(bf16[96,768]{1,0:T(8,128)(2,1)S(1)} %fusion.27), channel_id=1, source_target_pairs={{0,8},{4,12},{8,0},{12,4},{16,24},{20,28},{24,16},{28,20},{1,9},{5... | collective-permute-start | bytes 442376 | tf_op jit(solution)/shard_map/ppermute | solution.py:690
  294.2 16.8 %collective-permute-start.59 = (bf16[96,768]{1,0:T(8,128)(2,1)S(1)}, bf16[96,768]{1,0:T(8,128)(2,1)S(1)}, u32[]{:S(2)}, u32[]{:S(2)}) collective-permute-start(bf16[96,768]{1,0:T(8,128)(2,1)S(1)} %fusion.27), channel_id=1, source_target_pairs={{0,16},{4,20},{8,24},{12,28},{16,0},{20,4},{24,8},{28,12},{1,17},{... | collective-permute-start | bytes 442376 | tf_op jit(solution)/shard_map/ppermute | solution.py:690
  295.1 15.9 %collective-permute-start.60 = (bf16[96,768]{1,0:T(8,128)(2,1)S(1)}, bf16[96,768]{1,0:T(8,128)(2,1)S(1)}, u32[]{:S(2)}, u32[]{:S(2)}) collective-permute-start(bf16[96,768]{1,0:T(8,128)(2,1)S(1)} %fusion.27), channel_id=1, source_target_pairs={{0,24},{4,28},{8,16},{12,20},{16,8},{20,12},{24,0},{28,4},{1,25},{... | collective-permute-start | bytes 442376 | tf_op jit(solution)/shard_map/ppermute | solution.py:690
  296.3 5.9 %collective-permute-start.57 = (f32[5,768]{1,0:T(8,128)S(1)}, f32[5,768]{1,0:T(8,128)S(1)}, u32[]{:S(2)}, u32[]{:S(2)}) collective-permute-start(f32[5,768]{1,0:T(8,128)S(1)} %add.392), channel_id=1, source_target_pairs={{0,16},{4,20},{8,24},{12,28},{16,0},{20,4},{24,8},{28,12},{1,17},{... | collective-permute-start | bytes 46088 | tf_op jit(solution)/shard_map/ppermute | solution.py:690
  311.0 7.0 %collective-permute-start.61 = (bf16[4,96,768]{2,1,0:T(8,128)(2,1)S(1)}, bf16[4,96,768]{2,1,0:T(8,128)(2,1)S(1)}, u32[]{:S(2)}, u32[]{:S(2)}) collective-permute-start(bf16[4,96,768]{2,1,0:T(8,128)(2,1)S(1)} %pad_maximum_fusion.5.near), channel_id=1, source_target_pairs={{0,4},{4,0},{8,12},{12,8},{16,20},{20,16},{24,28},{28,24},{1,5},{5... | collective-permute-start | bytes 1769480 | tf_op jit(solution)/shard_map/ppermute | solution.py:690
  312.7 4.7 %collective-permute-start.62 = (f32[5,768]{1,0:T(8,128)S(1)}, f32[5,768]{1,0:T(8,128)S(1)}, u32[]{:S(2)}, u32[]{:S(2)}) collective-permute-start(f32[5,768]{1,0:T(8,128)S(1)} %add.393), channel_id=1, source_target_pairs={{0,4},{4,0},{8,12},{12,8},{16,20},{20,16},{24,28},{28,24},{1,5},{5... | collective-permute-start | bytes 46088 | tf_op jit(solution)/shard_map/ppermute | solution.py:690
  (41 other events, 328.2 us)
